TPU v7x, 256 devices: a whole 4x4x8 slice. The times are simulated.
256 devices in a mesh: tm: 8 (over x, y_hi), space: 32 (over y_lo, z, core).
Axes of the slice: x: 4, y: 4 (y_hi: 2, y_lo: 2; y = y_hi * 2 + y_lo), z: 8, core: 2. Of those that a mesh axis runs over, the one named last changes fastest.
Arguments:
- snapshots: bfloat16 [4096, 65536], P('tm', 'space'), may hold values from -13 to 13
- modes_basis: bfloat16 [65536, 64], P('space'), may hold values from -0.0234375 to 0.0234375
- reg_weights: float32 [2144], replicated, may hold values from 0.3 to 3
Outputs:
- reduced: float32 [4096, 64], P('tm')
- time_rates: float32 [4096, 64], P('tm')
- normal: float32 [2144, 2144], P('tm', 'space')
- right_side: float32 [2144, 64], P('tm')
All inputs are finite; a program needn't handle non-finite values.
Results may differ from a plain program's by a relative error of at most 0.0043.
Values sent between devices are 32-bit elements; how exact they have to be, the bound alone decides.
A program may use at most 128 MiB of HBM per device.

v0:
```python
import jax
import jax.numpy as jnp
from jax import lax
from jax.sharding import PartitionSpec as P


def with_halo(block, sides, width):
    for axis, dim in sides:
        count = lax.axis_size(axis)
        forward = [(i, i + 1) for i in range(count - 1)]
        backward = [(target, source) for source, target in forward]
        low = lax.ppermute(
            lax.slice_in_dim(block, block.shape[dim] - width, None, axis=dim), axis, forward
        )
        high = lax.ppermute(lax.slice_in_dim(block, 0, width, axis=dim), axis, backward)
        block = jnp.concatenate([low, block, high], axis=dim)
    return block


def features_of(reduced):
    pieces = [reduced]
    for column in range(reduced.shape[1]):
        pieces.append(reduced[:, column : column + 1] * reduced[:, column:])
    return jnp.concatenate(pieces, axis=1).astype(jnp.bfloat16)


def local(snapshots, modes_basis, reg_weights):
    feature_count = reg_weights.shape[0]
    snaps_dev = snapshots.shape[0]
    tm_count = lax.axis_size("tm")
    space_count = lax.axis_size("space")
    inv_count = 1.0 / (snaps_dev * tm_count)
    row_block = feature_count // tm_count
    col_block = feature_count // space_count
    time_idx = lax.axis_index("tm")
    space_idx = lax.axis_index("space")
    col_start = space_idx * col_block
    partial_value = jnp.dot(snapshots, modes_basis, preferred_element_type=jnp.float32)
    reduced = lax.psum(partial_value, "space")
    contract = (((0,), (0,)), ((), ()))
    padded = with_halo(reduced, (("tm", 0),), 1)
    central = (padded[2:] - padded[:-2]) * 0.5
    first_row = jnp.where(time_idx == 0, padded[2:3] - padded[1:2], central[0:1])
    last_row = jnp.where(time_idx == tm_count - 1, padded[-2:-1] - padded[-3:-2], central[-1:])
    time_rates = jnp.concatenate([first_row, central[1:-1], last_row], axis=0)
    features = features_of(reduced)
    rates_bf = time_rates.astype(jnp.bfloat16)
    own_cols = lax.dynamic_slice_in_dim(features, col_start, col_block, 1)
    right_block = jnp.concatenate([own_cols, rates_bf], axis=1)
    summed = lax.psum_scatter(
        lax.dot_general(features, right_block, contract, preferred_element_type=jnp.float32)
        * inv_count,
        "tm",
        scatter_dimension=0,
        tiled=True,
    )
    row_ids = time_idx * row_block + lax.broadcasted_iota(jnp.int32, (row_block, col_block), 0)
    col_ids = col_start + lax.broadcasted_iota(jnp.int32, (row_block, col_block), 1)
    reg_rows = lax.dynamic_slice_in_dim(reg_weights, time_idx * row_block, row_block, 0)
    normal = summed[:, :col_block] + jnp.where(row_ids == col_ids, reg_rows[:, None], 0.0)
    right_side = summed[:, col_block:]
    return (reduced, time_rates, normal, right_side)


def solution(mesh):
    return jax.shard_map(
        local,
        mesh=mesh,
        in_specs=(P("tm", "space"), P("space", None), P()),
        out_specs=(P("tm", None), P("tm", None), P("tm", "space"), P("tm", None)),
        check_vma=False,
    )
```

profile of v0, /device:TPU:32, one launch (start us, length us, event | category | flops | bytes accessed | tf_op | source)
XLA Modules:
  0.0 460.9 jit_solution(3846174341480016466)
XLA Ops:
  7.2 1.5 copy-done
  8.8 2.4 fusion.75
  11.2 199.8 %all-reduce.4.cloned.1.call-done = f32[512,64]{0,1:T(8,128)} async-done(((f32[512,64]{0,1:T(8,128)}), f32[512,64]{0,1:T(8,128)}) %all-reduce.4.cloned.1.call-update) | async-done | bytes 131088 | tf_op jit(solution)/shard_map/psum | solution.py:39
  211.0 0.9 fusion.74
  211.9 1.3 collective-permute-start
  213.2 6.1 %collective-permute-start.1 = (f32[1,64]{0,1:T(8,128)S(1)}, f32[1,64]{0,1:T(8,128)S(1)}, u32[]{:S(2)}, u32[]{:S(2)}) collective-permute-start(f32[1,64]{0,1:T(8,128)S(1)} %get-tuple-element.76), channel_id=1, source_target_pairs={{0,32},{32,64},{64,96},{96,128},{128,160},{160,192},{192,224},{1,3... | collective-permute-start | bytes 776 | tf_op jit(solution)/shard_map/ppermute | solution.py:12
  219.2 1.5 fusion.67
  220.7 1.2 fusion.72
  221.9 1.1 fusion.71
  223.0 1.2 fusion.70
  224.2 0.9 fusion.3
  225.1 0.9 fusion.4
  226.1 0.9 fusion.5
  227.0 0.9 fusion.6
  227.9 0.9 fusion.12
  228.8 0.9 fusion.13
  229.8 0.9 fusion.14
  230.7 0.9 fusion.15
  231.6 0.9 fusion.16
  233.2 0.6 fusion.21
  235.1 0.6 fusion.24
  235.8 0.6 fusion.25
  236.4 0.6 fusion.26
  261.2 86.8 %concatenate.20 = bf16[512,2144]{0,1:T(8,128)(2,1)} concatenate(bf16[512,64]{0,1:T(8,128)(2,1)S(1)} %get-tuple-element.73, bf16[512,64]{0,1:T(8,128)(2,1)S(1)} %get-tuple-element.72, bf16[512,63]{0,1:T(8,128)(2,1)S(1)} %fusion.9, bf16[512,62]{0,1:T(8,128)(2,1)S(1)} %fusion.8, bf16[512,61]{0,1:T(8,128)(2,1)S(1)} %fusion.7, bf16[512,60]{0,1:T(8,128)(2,1)S(1)} %fusion.6, ...), dimensions={1} | concatenate | bytes 4390912 | tf_op jit(solution)/shard_map/concatenate | solution.py:24
  348.0 0.9 constant_dynamic-slice_fusion
  349.0 0.8 fusion.69
  349.8 3.5 convolution_multiply_fusion
  353.3 0.8 dynamic_slice.7
  355.4 94.8 %all-reduce.6.cloned.1.call-done = f32[2144,131]{0,1:T(8,128)} async-done(((f32[2144,131]{0,1:T(8,128)}), f32[2144,131]{0,1:T(8,128)}) %all-reduce.6.cloned.1.call-update) | async-done | bytes 1123472
  450.1 1.6 dynamic-slice.3
  451.8 1.7 dynamic-slice_add_fusion
  453.5 0.7 copy.11
  (66 shorter events, 26.9 us)
Async XLA Ops:
  7.2 1.6 copy-start
  7.2 203.8 %all-reduce.4.cloned.1.call-start = ((), (), s32[]{:S(2)}) async-start(), calls=%async_computation | async-start | bytes 262144 | tf_op jit(solution)/shard_map/psum | solution.py:39
  11.2 439.0 %all-reduce.6.cloned.1.call-start = ((), (), s32[]{:S(2)}) async-start(), calls=%async_computation.1 | async-start | bytes 2367488
  211.0 21.6 %copy-start.1 = (f32[512,64]{0,1:T(8,128)S(1)}, f32[512,64]{0,1:T(8,128)}, u32[]{:S(2)}) copy-start(f32[512,64]{0,1:T(8,128)} %all-reduce.4.cloned.1.call-done) | copy-start | bytes 393220
  211.9 49.1 %collective-permute-start = (f32[1,64]{0,1:T(8,128)S(1)}, f32[1,64]{0,1:T(8,128)S(1)}, u32[]{:S(2)}, u32[]{:S(2)}) collective-permute-start(f32[1,64]{0,1:T(8,128)S(1)} %get-tuple-element.75), channel_id=1, source_target_pairs={{32,0},{64,32},{96,64},{128,96},{160,128},{192,160},{224,192},{33,... | collective-permute-start | bytes 776 | tf_op jit(solution)/shard_map/ppermute | solution.py:15
  213.2 47.8 %collective-permute-start.1 = (f32[1,64]{0,1:T(8,128)S(1)}, f32[1,64]{0,1:T(8,128)S(1)}, u32[]{:S(2)}, u32[]{:S(2)}) collective-permute-start(f32[1,64]{0,1:T(8,128)S(1)} %get-tuple-element.76), channel_id=1, source_target_pairs={{0,32},{32,64},{64,96},{96,128},{128,160},{160,192},{192,224},{1,3... | collective-permute-start | bytes 776 | tf_op jit(solution)/shard_map/ppermute | solution.py:12
  349.7 4.3 copy-start.2
Sparse Core Ops, SparseCore 0:
  11.3 199.6 all-reduce.3
  353.4 96.6 all-reduce.5
where the time goes:
time: 468 us; the launch traced here: 461 us
  waiting for transfers between devices  295 us (63%)
  local copies, waits for them, and re-layouts  97.4 us (21%)
  other arithmetic  40.8 us (9%)
  between operations  14.9 us (3%)
  starting transfers between devices  7.42 us (2%)
  matrix products  5.9 us (1%)
    psum x1, waiting for transfers between devices, local(): reduced = lax.psum(partial_value, 'space')  200 us
    unnamed x3, waiting for transfers between devices  94.8 us
    concatenate x1, local copies, waits for them, and re-layouts, features_of(): return jnp.concatenate(pieces, axis=1).astype(jnp.bfloat16)  86.8 us
    another operation x64, other arithmetic  38.2 us
  transfers between devices with their start and end apart: 4, of which 2 were waited for; matrix products, arithmetic and copies ran while one was open for 9% of the time, Pallas kernels for 0%

commit v1 on v0

v1 whole, which is shorter than its diff:
```python
import functools

import jax
import jax.numpy as jnp
from jax import lax
from jax.experimental import pallas as pl
from jax.experimental.pallas import tpu as pltpu
from jax.sharding import PartitionSpec as P

MESH = pl.DeviceIdType.MESH
F32 = jnp.float32
BF16 = jnp.bfloat16
CONTRACT = (((1,), (1,)), ((), ()))

NX, NY, NZ = 4, 4, 8
R = 64
FEATURES = 2144
SNAPS = 4096
GROUP = 512
LANES = 128
KB = GROUP // LANES
HALF = 256
ROWS = FEATURES // 8
COLS = FEATURES // 32
ROWS_P = 272
COLS_8 = 72
COLS_P = 2 * COLS_8
WIDE = 384
SEL = ROWS_P + COLS_P
OUT_N = COLS_P + R


def start_of(q):
    return R + R * q - (q * (q - 1)) // 2


def position():
    t, s = lax.axis_index("tm"), lax.axis_index("space")
    x, yh = t // 2, t % 2
    yl, z, c = s // 16, (s % 16) // 2, s % 2
    return t, s, x, yh * 2 + yl, z, c


def device_at(x, y, z, c):
    return (x * 2 + y // 2, (y % 2) * 16 + z * 2 + c)


def selectors(t, s, sel_ref):
    shape = (SEL, 256)
    row = lax.broadcasted_iota(jnp.int32, shape, 0)
    lane = lax.broadcasted_iota(jnp.int32, shape, 1)
    column = row - ROWS_P
    column = jnp.where(column < COLS_8, column, column - COLS_8 + COLS)
    f = jnp.where(row < ROWS_P, ROWS * t + row, 2 * COLS * (s // 2) + column)
    q = lane % R
    part = lane < 3 * R
    begin = start_of(q)
    linear = f < R
    first = (f >= begin) & (f < start_of(q + 1))
    first = ((linear & (f == q)) | first) & part
    count = jnp.sum(jnp.where((f >= begin) & (lane < R), 1.0, 0.0), axis=1, keepdims=True)
    i = count.astype(jnp.int32) - 1
    j = f - start_of(i) + i
    second = (linear & (lane == 3 * R)) | (~linear & (q == j) & part)
    sel_ref[:SEL, :] = jnp.where(first, 1.0, 0.0).astype(BF16)
    sel_ref[SEL:, :] = jnp.where(second, 1.0, 0.0).astype(BF16)


def kernel(
    snap_hbm, basis_hbm, reg_hbm,
    red_ref, rate_ref, norm_ref, rhs_ref,
    snap_v, basis_v, reg_s, pbuf, rbuf, gbuf, sel, edge, oedge, rates, acc, oacc, norm_v, rhs_v,
    in_sem, rs_send, rs_recv, g1_send, g1_recv, g2_send, g2_recv, g3_send, g3_recv, x_send, x_recv, out_sem,
):
    t, s, x, y, z, c = position()
    yl = y % 2
    me = 4 * x + y
    other = device_at(x, y, z, 1 - c)

    basis_in = pltpu.make_async_copy(basis_hbm, basis_v, in_sem.at[KB])
    basis_in.start()
    snaps_in = []
    for kb in range(KB):
        rows = pl.ds(kb * LANES, LANES)
        copy = pltpu.make_async_copy(snap_hbm.at[rows], snap_v.at[rows], in_sem.at[kb])
        copy.start()
        snaps_in.append(copy)
    reg_in = pltpu.make_async_copy(reg_hbm, reg_s, in_sem.at[KB + 1])
    reg_in.start()

    barrier = pltpu.get_barrier_semaphore()
    for d in range(1, 32):
        pl.semaphore_signal(barrier, inc=1, device_id=(t, (s + d) % 32), device_id_type=MESH)
    for d in range(1, NX):
        pl.semaphore_signal(barrier, inc=1, device_id=device_at((x + d) % NX, y, z, c), device_id_type=MESH)
    for d in range(2):
        pl.semaphore_signal(
            barrier, inc=1, device_id=device_at(x, (y // 2 * 2 + 2) % 4 + d, z, c), device_id_type=MESH
        )

    basis_in.wait()
    for kb in range(KB):
        snaps_in[kb].wait()
        pbuf[kb] = lax.dot_general(
            basis_v[...], snap_v[kb * LANES:(kb + 1) * LANES, :], CONTRACT, preferred_element_type=F32
        )
        if kb == 0:
            pl.semaphore_wait(barrier, 36)
        for d in range(NZ):
            zz = (z + d) % NZ
            to = (kb % 2) * 16 + zz * 2 + kb // 2
            copy = pltpu.make_async_remote_copy(
                src_ref=pbuf.at[kb, pl.ds(pl.multiple_of(8 * zz, 8), 8)],
                dst_ref=rbuf.at[(s - to + 32) % 32],
                send_sem=rs_send, recv_sem=rs_recv,
                device_id=(t, to), device_id_type=MESH,
            )
            if d == 0:
                pl.when(to != s)(copy.start)
            else:
                copy.start()

    selectors(t, s, sel)
    reg_in.wait()

    pltpu.make_async_remote_copy(
        src_ref=rbuf.at[pl.ds(1, 31)], dst_ref=rbuf.at[pl.ds(1, 31)],
        send_sem=rs_send, recv_sem=rs_recv, device_id=other, device_id_type=MESH,
    ).wait()
    zrows = pl.ds(pl.multiple_of(8 * z, 8), 8)
    total = pbuf[2 * c + yl, zrows, :]
    for d in range(1, 32):
        total = total + rbuf[d]
    gbuf[me, zrows, :] = total

    for d in range(1, NZ):
        pltpu.make_async_remote_copy(
            src_ref=gbuf.at[me, zrows], dst_ref=gbuf.at[me, zrows],
            send_sem=g1_send, recv_sem=g1_recv,
            device_id=device_at(x, y, (z + d) % NZ, c), device_id_type=MESH,
        ).start()
    pltpu.make_async_remote_copy(
        src_ref=gbuf.at[me, pl.ds(0, 56)], dst_ref=gbuf.at[me, pl.ds(0, 56)],
        send_sem=g1_send, recv_sem=g1_recv, device_id=other, device_id_type=MESH,
    ).wait()

    def along_x(ref, d, sems):
        return pltpu.make_async_remote_copy(
            src_ref=ref, dst_ref=ref, send_sem=sems[0], recv_sem=sems[1],
            device_id=device_at((x + d) % NX, y, z, c), device_id_type=MESH,
        )

    def along_y(ref, d, sems):
        return pltpu.make_async_remote_copy(
            src_ref=ref, dst_ref=ref, send_sem=sems[0], recv_sem=sems[1],
            device_id=device_at(x, (y + d) % NY, z, c), device_id_type=MESH,
        )

    first_hop = []
    for d in (1, 3, 2):
        for k, along in enumerate((along_x, along_y)):
            copy = along(gbuf.at[me], d, (g2_send.at[k, d], g2_recv.at[k, d]))
            copy.start()
            first_hop.append(copy)
    for d in (1, 3, 2):
        along_x(gbuf.at[me], d, (g2_send.at[0, d], g2_recv.at[0, d])).wait_recv()
        source = 4 * ((x - d + NX) % NX) + y
        for e in (1, 3, 2):
            along_y(gbuf.at[source, pl.ds(0, 32)], e, (g3_send, g3_recv)).start()
        along_y(gbuf.at[me], d, (g2_send.at[1, d], g2_recv.at[1, d])).wait_recv()
        source = 4 * x + (y - d + NY) % NY
        for e in (1, 3, 2):
            along_x(gbuf.at[source, pl.ds(32, 32)], e, (g3_send, g3_recv)).start()
    for copy in first_hop:
        copy.wait_send()
    along_x(gbuf.at[pl.ds(0, 9)], 1, (g3_send, g3_recv)).wait()

    def across(src, dst, k):
        return pltpu.make_async_remote_copy(
            src_ref=src, dst_ref=dst, send_sem=x_send.at[k], recv_sem=x_recv.at[k],
            device_id=other, device_id_type=MESH,
        )

    lane = lax.broadcasted_iota(jnp.int32, (R, LANES), 1)
    edges = jnp.zeros((R, LANES), F32)
    for g in range(8):
        edges = jnp.where(lane == 2 * g, gbuf[2 * g][:, 0:1], edges)
        edges = jnp.where(lane == 2 * g + 1, gbuf[2 * g + 1][:, LANES - 1:], edges)
    edge[...] = edges
    send_edge = across(edge, oedge, 0)
    send_edge.start()
    outs = []
    for h in range(2):
        mine = red_ref.at[:, pl.ds(pl.multiple_of(c * HALF + h * LANES, LANES), LANES)]
        copy = across(gbuf.at[2 * t + h], mine, 1 + h)
        copy.start()
        outs.append(copy)
        copy = pltpu.make_async_copy(gbuf.at[2 * t + h], mine, out_sem.at[h])
        copy.start()
        outs.append(copy)
    send_edge.wait()

    got = oedge[...]
    left = jnp.where(c == 0, pltpu.roll(got, 2, 1), got)
    right = jnp.where(c == 0, got, pltpu.roll(got, LANES - 2, 1))
    lane = lax.broadcasted_iota(jnp.int32, (R, HALF), 1)
    for g in range(8):
        r = jnp.concatenate([gbuf[2 * g], gbuf[2 * g + 1]], axis=1)
        before = jnp.where(lane == 0, left[:, 2 * g + 1:2 * g + 2], pltpu.roll(r, 1, 1))
        after = jnp.where(lane == HALF - 1, right[:, 2 * g:2 * g + 1], pltpu.roll(r, HALF - 1, 1))
        rate = (after - before) * 0.5
        if g == 0:
            rate = jnp.where((lane == 0) & (c == 0), after - r, rate)
        if g == 7:
            rate = jnp.where((lane == HALF - 1) & (c == 1), r - before, rate)
        rates[g] = rate
    mine = rate_ref.at[:, pl.ds(pl.multiple_of(c * HALF, HALF), HALF)]
    copy = across(rates.at[t], mine, 3)
    copy.start()
    outs.append(copy)
    copy = pltpu.make_async_copy(rates.at[t], mine, out_sem.at[2])
    copy.start()
    outs.append(copy)

    acc[...] = jnp.zeros_like(acc)
    ones = jnp.where(lax.broadcasted_iota(jnp.int32, (R, HALF), 0) == 0, 1.0, 0.0).astype(BF16)

    def products(g, carry):
        r = jnp.concatenate([gbuf[2 * g], gbuf[2 * g + 1]], axis=1)
        high = r.astype(BF16)
        rest = r - high.astype(F32)
        middle = rest.astype(BF16)
        low = (rest - middle.astype(F32)).astype(BF16)
        parts = jnp.concatenate([high, middle, low, ones], axis=0)
        picked = jnp.dot(sel[...], parts, preferred_element_type=F32)
        feature = (picked[:SEL] * picked[SEL:]).astype(BF16)
        columns = jnp.concatenate([feature[ROWS_P:], rates[g].astype(BF16)], axis=0)
        acc[:, :ROWS_P] += lax.dot_general(
            columns, feature[:ROWS_P], CONTRACT, preferred_element_type=F32
        )
        return carry

    lax.fori_loop(0, 8, products, 0)
    theirs = pl.ds(pl.multiple_of((1 - c) * COLS_8, 8), COLS_8)
    send_norm = across(acc.at[theirs], oacc.at[pl.ds(0, COLS_8)], 4)
    send_norm.start()
    send_rhs = across(acc.at[pl.ds(COLS_P, R)], oacc.at[pl.ds(COLS_8, R)], 5)
    send_rhs.start()

    spot = COLS * (s % 4)
    lane = lax.broadcasted_iota(jnp.int32, (8, WIDE), 1)

    def pick_weight(i, v):
        return jnp.where(lane == spot + i, reg_s[COLS * s + i], v)

    weight = lax.fori_loop(0, COLS, pick_weight, jnp.zeros((8, WIDE), F32))
    column = lax.broadcasted_iota(jnp.int32, (COLS, ROWS), 0)
    row = lax.broadcasted_iota(jnp.int32, (COLS, ROWS), 1)
    diagonal = (ROWS * t + row) == (COLS * s + column)

    send_norm.wait()
    mine = pl.ds(pl.multiple_of(c * COLS_8, 8), COLS_8)
    summed = (acc[mine, :] + oacc[:COLS_8, :]) * (1.0 / SNAPS)
    norm_v[...] = summed[:COLS, :ROWS] + jnp.where(diagonal, weight[0:1, :ROWS], 0.0)
    copy = pltpu.make_async_copy(norm_v, norm_ref, out_sem.at[3])
    copy.start()
    outs.append(copy)
    send_rhs.wait()
    summed = (acc[COLS_P:, :] + oacc[COLS_8:, :]) * (1.0 / SNAPS)
    rhs_v[...] = summed[:, :ROWS]
    copy = pltpu.make_async_copy(rhs_v, rhs_ref, out_sem.at[4])
    copy.start()
    outs.append(copy)
    for copy in outs:
        copy.wait()


def local(snapshots, modes_basis, reg_weights):
    f32 = lambda *shape: pltpu.VMEM(shape, F32)
    dma = pltpu.SemaphoreType.DMA
    outs = pl.pallas_call(
        kernel,
        out_shape=(
            jax.ShapeDtypeStruct((R, GROUP), F32),
            jax.ShapeDtypeStruct((R, GROUP), F32),
            jax.ShapeDtypeStruct((COLS, ROWS), F32),
            jax.ShapeDtypeStruct((R, ROWS), F32),
        ),
        in_specs=[pl.BlockSpec(memory_space=pltpu.HBM)] * 3,
        out_specs=[pl.BlockSpec(memory_space=pltpu.HBM)] * 4,
        scratch_shapes=[
            pltpu.VMEM((GROUP, 2048), BF16),
            pltpu.VMEM((R, 2048), BF16),
            pltpu.SMEM((FEATURES,), F32),
            f32(KB, R, LANES),
            f32(32, 8, LANES),
            f32(16, R, LANES),
            pltpu.VMEM((2 * SEL, 256), BF16),
            f32(R, LANES),
            f32(R, LANES),
            f32(8, R, HALF),
            f32(OUT_N, WIDE),
            f32(COLS_8 + R, WIDE),
            f32(COLS, ROWS),
            f32(R, ROWS),
            dma((KB + 2,)),
            dma, dma,
            dma, dma,
            dma((2, 4)), dma((2, 4)),
            dma, dma,
            dma((6,)), dma((6,)),
            dma((5,)),
        ],
        compiler_params=pltpu.CompilerParams(
            collective_id=0, has_side_effects=True, vmem_limit_bytes=32 * 1024 * 1024
        ),
        cost_estimate=pl.CostEstimate(flops=1 << 30, bytes_accessed=3 << 20, transcendentals=0),
    )(snapshots, modes_basis.T, reg_weights)
    return tuple(out.T for out in outs)


def solution(mesh):
    return jax.shard_map(
        local,
        mesh=mesh,
        in_specs=(P("tm", "space"), P("space", None), P()),
        out_specs=(P("tm", None), P("tm", None), P("tm", "space"), P("tm", None)),
        check_vma=False,
    )
```

time: 468 us -> 46 us (0.10)
  the two profiles are of different devices: /device:TPU:32 before, /device:TPU:1 now
where the time goes in v1:
time: 46 us; the launch traced here: 45.8 us
  Pallas kernels  39.3 us (85%)
  local copies, waits for them, and re-layouts  5.84 us (13%)
  between operations  0.65 us (1%)
    pallas_call x1, Pallas kernels, local(): pl.pallas_call(kernel, out_shape=(jax.ShapeDtypeStruct((R, GROUP), F32),...  39.3 us
    unnamed x10, local copies, waits for them, and re-layouts  5.84 us

profile of v1, /device:TPU:1, one launch (start us, length us, event | category | flops | bytes accessed | tf_op | source)
XLA Modules:
  0.0 45.8 jit_solution(7544226871360294050)
XLA Ops:
  0.6 0.0 copy-start
  0.6 1.6 %copy-done = bf16[512,2048]{1,0:T(8,128)(2,1)S(1)} copy-done((bf16[512,2048]{1,0:T(8,128)(2,1)S(1)}, bf16[512,2048]{1,0:T(8,128)(2,1)}, u32[]{:S(2)}) %copy-start) | copy-done | bytes 2097176
  2.2 0.0 copy-start.1
  2.2 0.9 %copy-done.1 = bf16[2048,64]{0,1:T(8,128)(2,1)S(1)} copy-done((bf16[2048,64]{0,1:T(8,128)(2,1)S(1)}, bf16[2048,64]{0,1:T(8,128)(2,1)}, u32[]{:S(2)}) %copy-start.1) | copy-done | bytes 262168
  3.2 0.0 copy-start.2
  3.2 0.7 %copy-done.2 = f32[2144]{0:T(1024)S(1)} copy-done((f32[2144]{0:T(1024)S(1)}, f32[2144]{0:T(1024)}, u32[]{:S(2)}) %copy-start.2) | copy-done | bytes 8600
  3.9 39.3 %shard_map.66 = (f32[64,512]{1,0:T(8,128)S(1)}, f32[64,512]{1,0:T(8,128)S(1)}, f32[67,268]{1,0:T(8,128)S(1)}, f32[64,268]{1,0:T(8,128)S(1)}) custom-call(bf16[512,2048]{1,0:T(8,128)(2,1)S(1)} %copy-done, bf16[64,2048]{1,0:T(8,128)(2,1)S(1)} %bitcast.9, f32[2144]{0:T(1024)S(1)} %copy-done.2), custom_call_target="tpu_custom_call" | custom-call | flops 1073741824 | bytes 3145728 | tf_op jit(solution)/shard_map/pallas_call | solution.py:281
  43.2 0.7 %copy.11 = f32[512,64]{0,1:T(8,128)} copy(f32[512,64]{0,1:T(8,128)S(1)} %bitcast.6) | data formatting | bytes 262144
  43.9 0.7 %copy.12 = f32[512,64]{0,1:T(8,128)} copy(f32[512,64]{0,1:T(8,128)S(1)} %bitcast.5) | data formatting | bytes 262144
  44.5 0.6 %copy.13 = f32[268,67]{0,1:T(8,128)} copy(f32[268,67]{0,1:T(8,128)S(1)} %bitcast.7) | data formatting | bytes 143648
  45.2 0.6 %copy.14 = f32[268,64]{0,1:T(8,128)} copy(f32[268,64]{0,1:T(8,128)S(1)} %bitcast.8) | data formatting | bytes 137216
Async XLA Ops:
  0.6 1.6 %copy-start = (bf16[512,2048]{1,0:T(8,128)(2,1)S(1)}, bf16[512,2048]{1,0:T(8,128)(2,1)}, u32[]{:S(2)}) copy-start(bf16[512,2048]{1,0:T(8,128)(2,1)} %snap_hbm.1) | copy-start | bytes 6291460
  2.2 0.9 %copy-start.1 = (bf16[2048,64]{0,1:T(8,128)(2,1)S(1)}, bf16[2048,64]{0,1:T(8,128)(2,1)}, u32[]{:S(2)}) copy-start(bf16[2048,64]{0,1:T(8,128)(2,1)} %param.4) | copy-start | bytes 786436
  3.2 0.7 %copy-start.2 = (f32[2144]{0:T(1024)S(1)}, f32[2144]{0:T(1024)}, u32[]{:S(2)}) copy-start(f32[2144]{0:T(1024)} %reg_hbm.1) | copy-start | bytes 25732

commit v2 on v1

v2 whole, which is shorter than its diff:
```python
import functools

import jax
import jax.numpy as jnp
from jax import lax
from jax.experimental import pallas as pl
from jax.experimental.pallas import tpu as pltpu
from jax.sharding import PartitionSpec as P

MESH = pl.DeviceIdType.MESH
F32 = jnp.float32
BF16 = jnp.bfloat16
CONTRACT = (((1,), (1,)), ((), ()))

NX, NY, NZ = 4, 4, 8
R = 64
FEATURES = 2144
SNAPS = 4096
GROUP = 512
LANES = 128
KB = GROUP // LANES
HALF = 256
ROWS = FEATURES // 8
COLS = FEATURES // 32
ROWS_P = 272
COLS_8 = 72
COLS_P = 2 * COLS_8
WIDE = 384
SEL = ROWS_P + COLS_P
XY_ORDER = [(dx, dy) for dx in (0, 1, 3, 2) for dy in (0, 1, 3, 2) if dx or dy]
Z_ORDER = (1, 7, 2, 6, 3, 5, 4)


def start_of(q):
    return R + R * q - (q * (q - 1)) // 2


def position():
    t, s = lax.axis_index("tm"), lax.axis_index("space")
    x, yh = t // 2, t % 2
    yl, z, c = s // 16, (s % 16) // 2, s % 2
    return t, s, x, yh * 2 + yl, z, c


def device_at(x, y, z, c):
    return (x * 2 + y // 2, (y % 2) * 16 + z * 2 + c)


def selectors(t, s, sel_ref):
    shape = (SEL, 256)
    row = lax.broadcasted_iota(jnp.int32, shape, 0)
    lane = lax.broadcasted_iota(jnp.int32, shape, 1)
    column = row - ROWS_P
    column = jnp.where(column < COLS_8, column, column - COLS_8 + COLS)
    f = jnp.where(row < ROWS_P, ROWS * t + row, 2 * COLS * (s // 2) + column)
    q = lane % R
    part = lane < 3 * R
    begin = start_of(q)
    linear = f < R
    first = (f >= begin) & (f < start_of(q + 1))
    first = ((linear & (f == q)) | first) & part
    count = jnp.sum(jnp.where((f >= begin) & (lane < R), 1.0, 0.0), axis=1, keepdims=True)
    i = count.astype(jnp.int32) - 1
    j = f - start_of(i) + i
    second = (linear & (lane == 3 * R)) | (~linear & (q == j) & part)
    sel_ref[:SEL, :] = jnp.where(first, 1.0, 0.0).astype(BF16)
    sel_ref[SEL:, :] = jnp.where(second, 1.0, 0.0).astype(BF16)


def kernel(
    snap_hbm, basis_hbm, reg_hbm,
    red_ref, rate_ref, norm_ref, rhs_ref,
    snap_v, basis_v, reg_s, pbuf, rbuf, gbuf, obuf, sel, rates, rates_bf, feats, acc, rhs, oacc,
    in_sem, rs_send, rs_recv, g1_send, g1_recv, g2_send, g2_recv, f_send, f_recv, x_send, x_recv, out_sem,
):
    t, s, x, y, z, c = position()
    yl = y % 2
    me = 4 * x + y
    other = device_at(x, y, z, 1 - c)

    basis_in = pltpu.make_async_copy(basis_hbm, basis_v, in_sem.at[KB])
    basis_in.start()
    snaps_in = []
    for kb in range(KB):
        rows = pl.ds(kb * LANES, LANES)
        copy = pltpu.make_async_copy(snap_hbm.at[rows], snap_v.at[rows], in_sem.at[kb])
        copy.start()
        snaps_in.append(copy)
    reg_in = pltpu.make_async_copy(reg_hbm, reg_s, in_sem.at[KB + 1])
    reg_in.start()

    barrier = pltpu.get_barrier_semaphore()
    for d in range(1, 32):
        pl.semaphore_signal(barrier, inc=1, device_id=(t, (s + d) % 32), device_id_type=MESH)
    for dx in range(NX):
        for dy in range(NY):
            peer = device_at((x + dx) % NX, (y + dy) % NY, z, c)
            if dx:
                pl.semaphore_signal(barrier, inc=1, device_id=peer, device_id_type=MESH)
    for d in range(2):
        pl.semaphore_signal(
            barrier, inc=1, device_id=device_at(x, (y // 2 * 2 + 2) % 4 + d, z, c), device_id_type=MESH
        )

    basis_in.wait()
    for kb in range(KB):
        snaps_in[kb].wait()
        pbuf[kb] = lax.dot_general(
            basis_v[...], snap_v[kb * LANES:(kb + 1) * LANES, :], CONTRACT, preferred_element_type=F32
        )
        if kb == 0:
            pl.semaphore_wait(barrier, 31 + 12 + 2)
        for d in range(NZ):
            zz = (z + d) % NZ
            to = (kb % 2) * 16 + zz * 2 + kb // 2
            copy = pltpu.make_async_remote_copy(
                src_ref=pbuf.at[kb, pl.ds(pl.multiple_of(8 * zz, 8), 8)],
                dst_ref=rbuf.at[(s - to + 32) % 32],
                send_sem=rs_send, recv_sem=rs_recv,
                device_id=(t, to), device_id_type=MESH,
            )
            if d == 0:
                pl.when(to != s)(copy.start)
            else:
                copy.start()

    reg_in.wait()
    selectors(t, s, sel)

    spot = COLS * (s % 4)
    lane = lax.broadcasted_iota(jnp.int32, (8, WIDE), 1)

    def pick_weight(i, v):
        return jnp.where(lane == spot + i, reg_s[COLS * s + i], v)

    weight = lax.fori_loop(0, COLS, pick_weight, jnp.zeros((8, WIDE), F32))
    acc[...] = jnp.zeros_like(acc)

    pltpu.make_async_remote_copy(
        src_ref=rbuf.at[pl.ds(1, 31)], dst_ref=rbuf.at[pl.ds(1, 31)],
        send_sem=rs_send, recv_sem=rs_recv, device_id=other, device_id_type=MESH,
    ).wait()
    zrows = pl.ds(pl.multiple_of(8 * z, 8), 8)
    total = pbuf[2 * c + yl, zrows, :]
    for d in range(1, 32):
        total = total + rbuf[d]
    gbuf[me, zrows, :] = total

    def tile(zz):
        return gbuf.at[me, pl.ds(pl.multiple_of(8 * zz, 8), 8)]

    def along_z(d):
        return pltpu.make_async_remote_copy(
            src_ref=tile(z), dst_ref=tile(z), send_sem=g1_send, recv_sem=g1_recv.at[d],
            device_id=device_at(x, y, (z + d) % NZ, c), device_id_type=MESH,
        )

    def over_xy(zz):
        for dx, dy in XY_ORDER:
            pltpu.make_async_remote_copy(
                src_ref=tile(zz), dst_ref=tile(zz), send_sem=g2_send, recv_sem=g2_recv.at[4 * dx + dy],
                device_id=device_at((x + dx) % NX, (y + dy) % NY, z, c), device_id_type=MESH,
            ).start()

    for d in Z_ORDER:
        along_z(d).start()
    over_xy(z)
    for d in Z_ORDER:
        along_z(d).wait_recv()
        over_xy((z - d + NZ) % NZ)
    pltpu.make_async_remote_copy(
        src_ref=gbuf.at[me, pl.ds(0, 56)], dst_ref=gbuf.at[me, pl.ds(0, 56)],
        send_sem=g1_send, recv_sem=g1_recv.at[0], device_id=other, device_id_type=MESH,
    ).wait_send()

    def across(src, dst, sems):
        return pltpu.make_async_remote_copy(
            src_ref=src, dst_ref=dst, send_sem=sems[0], recv_sem=sems[1],
            device_id=other, device_id_type=MESH,
        )

    ones = jnp.where(lax.broadcasted_iota(jnp.int32, (R, HALF), 0) == 0, 1.0, 0.0).astype(BF16)

    def products(n, carry):
        k = n // 2
        dx = k + k // 2 - 2 * (k // 3)
        xx = (x - dx + NX) % NX
        yh = (y // 2 + n) % 2
        for h in range(2):
            dy = (y - 2 * yh - h + NY) % NY
            source = 4 * xx + 2 * yh + h
            arrived = pltpu.make_async_remote_copy(
                src_ref=gbuf.at[source], dst_ref=gbuf.at[source], send_sem=g2_send, recv_sem=g2_recv.at[4 * dx + dy],
                device_id=other, device_id_type=MESH,
            )
            pl.when(source != me)(arrived.wait_recv)
        g = 2 * xx + yh
        both = pl.ds(2 * g, 2)
        across(gbuf.at[both], obuf.at[both], (f_send, f_recv)).start()
        r = jnp.concatenate([gbuf[2 * g], gbuf[2 * g + 1]], axis=1)
        rates[g] = (pltpu.roll(r, HALF - 1, 1) - pltpu.roll(r, 1, 1)) * 0.5
        high = r.astype(BF16)
        rest = r - high.astype(F32)
        middle = rest.astype(BF16)
        low = (rest - middle.astype(F32)).astype(BF16)
        parts = jnp.concatenate([high, middle, low, ones], axis=0)
        picked = jnp.dot(sel[...], parts, preferred_element_type=F32)
        feature = (picked[:SEL] * picked[SEL:]).astype(BF16)
        feats[:, pl.ds(pl.multiple_of(g * HALF, HALF), HALF)] = feature[:ROWS_P]
        acc[:, :ROWS_P] += lax.dot_general(
            feature[ROWS_P:], feature[:ROWS_P], CONTRACT, preferred_element_type=F32
        )
        return carry

    lax.fori_loop(0, 8, products, 0)
    theirs = pl.ds(pl.multiple_of((1 - c) * COLS_8, 8), COLS_8)
    send_norm = across(acc.at[theirs], oacc.at[pl.ds(0, COLS_8)], (x_send.at[0], x_recv.at[0]))
    send_norm.start()
    pltpu.make_async_remote_copy(
        src_ref=gbuf.at[pl.ds(0, 15)], dst_ref=gbuf.at[pl.ds(0, 15)],
        send_sem=g2_send, recv_sem=g1_recv.at[0], device_id=other, device_id_type=MESH,
    ).wait_send()

    across(gbuf, obuf, (f_send, f_recv)).wait()
    lane = lax.broadcasted_iota(jnp.int32, (R, LANES), 1)

    def edges(g, carry):
        low, high = gbuf[2 * g], gbuf[2 * g + 1]
        before = pltpu.roll(obuf[(2 * g - 1 + 2 * c + 16) % 16], 1, 1)
        after = pltpu.roll(obuf[(2 * g + 2 * c) % 16], LANES - 1, 1)
        second = pltpu.roll(low, LANES - 1, 1)
        last = pltpu.roll(high, 1, 1)
        first_rate = jnp.where((g == 0) & (c == 0), second - low, (second - before) * 0.5)
        last_rate = jnp.where((g == 7) & (c == 1), high - last, (after - last) * 0.5)
        first_rate = jnp.where(lane == 0, first_rate, rates[g, :, :LANES])
        last_rate = jnp.where(lane == LANES - 1, last_rate, rates[g, :, LANES:])
        rates[g, :, :LANES] = first_rate
        rates[g, :, LANES:] = last_rate
        start = pl.multiple_of(g * HALF, HALF)
        rates_bf[:, pl.ds(start, LANES)] = first_rate.astype(BF16)
        rates_bf[:, pl.ds(start + LANES, LANES)] = last_rate.astype(BF16)
        return carry

    lax.fori_loop(0, 8, edges, 0)
    rhs[:, :ROWS_P] = lax.dot_general(rates_bf[...], feats[...], CONTRACT, preferred_element_type=F32)
    send_rhs = across(rhs, oacc.at[pl.ds(COLS_8, R)], (x_send.at[1], x_recv.at[1]))
    send_rhs.start()

    outs = []
    mine = pl.ds(pl.multiple_of(c * HALF, HALF), HALF)
    send_rate = across(rates.at[t], rate_ref.at[:, mine], (x_send.at[2], x_recv.at[2]))
    send_rate.start()
    copy = pltpu.make_async_copy(rates.at[t], rate_ref.at[:, mine], out_sem.at[0])
    copy.start()
    outs.append(copy)
    for h in range(2):
        for k, (buf, core) in enumerate(((gbuf, c), (obuf, 1 - c))):
            lanes = pl.ds(pl.multiple_of(core * HALF + h * LANES, LANES), LANES)
            copy = pltpu.make_async_copy(buf.at[2 * t + h], red_ref.at[:, lanes], out_sem.at[1 + 2 * h + k])
            copy.start()
            outs.append(copy)

    column = lax.broadcasted_iota(jnp.int32, (COLS, ROWS), 0)
    row = lax.broadcasted_iota(jnp.int32, (COLS, ROWS), 1)
    diagonal = (ROWS * t + row) == (COLS * s + column)
    send_norm.wait()
    summed = (acc[pl.ds(pl.multiple_of(c * COLS_8, 8), COLS_8), :] + oacc[:COLS_8, :]) * (1.0 / SNAPS)
    norm_ref[...] = summed[:COLS, :ROWS] + jnp.where(diagonal, weight[0:1, :ROWS], 0.0)
    send_rate.wait()
    for copy in outs:
        copy.wait()
    send_rhs.wait()
    summed = (rhs[...] + oacc[COLS_8:, :]) * (1.0 / SNAPS)
    rhs_ref[...] = summed[:, :ROWS]


def write(red, rate, norm, rhs, red_out, rate_out, norm_out, rhs_out, sem):
    pairs = ((red, red_out), (rate, rate_out), (norm, norm_out), (rhs, rhs_out))
    copies = [pltpu.make_async_copy(a, b, sem.at[k]) for k, (a, b) in enumerate(pairs)]
    for copy in copies:
        copy.start()
    for copy in copies:
        copy.wait()


def local(snapshots, modes_basis, reg_weights):
    f32 = lambda *shape: pltpu.VMEM(shape, F32)
    bf16 = lambda *shape: pltpu.VMEM(shape, BF16)
    dma = pltpu.SemaphoreType.DMA
    shapes = ((R, GROUP), (R, GROUP), (COLS, ROWS), (R, ROWS))
    in_hbm = lambda a: pltpu.with_memory_space_constraint(a, pltpu.HBM)
    in_vmem = lambda a: pltpu.with_memory_space_constraint(a, pltpu.VMEM)
    outs = pl.pallas_call(
        kernel,
        out_shape=tuple(f32(*shape) for shape in shapes),
        in_specs=[pl.BlockSpec(memory_space=pltpu.HBM)] * 3,
        out_specs=[pl.BlockSpec(memory_space=pltpu.VMEM)] * 4,
        scratch_shapes=[
            bf16(GROUP, 2048),
            bf16(R, 2048),
            pltpu.SMEM((FEATURES,), F32),
            f32(KB, R, LANES),
            f32(32, 8, LANES),
            f32(16, R, LANES),
            f32(16, R, LANES),
            bf16(2 * SEL, 256),
            f32(8, R, HALF),
            bf16(R, 8 * HALF),
            bf16(ROWS_P, 8 * HALF),
            f32(COLS_P, WIDE),
            f32(R, WIDE),
            f32(COLS_8 + R, WIDE),
            dma((KB + 2,)),
            dma, dma,
            dma, dma((NZ,)),
            dma, dma((16,)),
            dma, dma,
            dma((3,)), dma((3,)),
            dma((5,)),
        ],
        compiler_params=pltpu.CompilerParams(
            collective_id=0, has_side_effects=True, vmem_limit_bytes=32 * 1024 * 1024
        ),
        cost_estimate=pl.CostEstimate(flops=1 << 30, bytes_accessed=3 << 20, transcendentals=0),
    )(in_hbm(snapshots), in_hbm(modes_basis.T), in_hbm(reg_weights))
    outs = pl.pallas_call(
        write,
        out_shape=tuple(jax.ShapeDtypeStruct(shape, F32) for shape in shapes),
        in_specs=[pl.BlockSpec(memory_space=pltpu.VMEM)] * 4,
        out_specs=[pl.BlockSpec(memory_space=pltpu.HBM)] * 4,
        scratch_shapes=[dma((4,))],
        compiler_params=pltpu.CompilerParams(vmem_limit_bytes=4 * 1024 * 1024),
    )(*[in_vmem(out) for out in outs])
    return tuple(out.T for out in outs)


def solution(mesh):
    return jax.shard_map(
        local,
        mesh=mesh,
        in_specs=(P("tm", "space"), P("space", None), P()),
        out_specs=(P("tm", None), P("tm", None), P("tm", "space"), P("tm", None)),
        check_vma=False,
    )
```

time: 46 us -> 36.7 us (0.80)
  local copies, waits for them, and re-layouts: 5.84 us -> 0 us
  Pallas kernels: 39.3 us -> 36 us
    unnamed x10 -> x0, local copies, waits for them, and re-layouts: 5.84 us -> none
    pallas_call x1 -> x2, Pallas kernels: 39.3 us -> 36 us  [the longest x1 35.2 us: local(): pl.pallas_call(kernel, out_shape=tuple((f32(*shape) for shape in shapes))...]
where the time goes in v2:
time: 36.7 us; the launch traced here: 36.6 us
  Pallas kernels  36 us (98%)
  between operations  0.64 us (2%)
    pallas_call x1, Pallas kernels, local(): pl.pallas_call(kernel, out_shape=tuple((f32(*shape) for shape in shapes))...  35.2 us
    pallas_call x1, Pallas kernels, local(): pl.pallas_call(write, out_shape=tuple((jax.ShapeDtypeStruct(shape, F32) f...  0.8 us

profile of v2, /device:TPU:1, one launch (start us, length us, event | category | flops | bytes accessed | tf_op | source)
XLA Modules:
  0.0 36.6 jit_solution(2206505684374842867)
XLA Ops:
  0.6 35.2 %shard_map.66 = (f32[64,512]{1,0:T(8,128)S(1)}, f32[64,512]{1,0:T(8,128)S(1)}, f32[67,268]{1,0:T(8,128)S(1)}, f32[64,268]{1,0:T(8,128)S(1)}) custom-call(bf16[512,2048]{1,0:T(8,128)(2,1)} %snap_hbm.1, bf16[64,2048]{1,0:T(8,128)(2,1)} %bitcast.5, f32[2144]{0:T(1024)} %reg_hbm.1), custom_call_target="tpu_custom_call" | custom-call | flops 1073741824 | bytes 3145728 | tf_op jit(solution)/shard_map/pallas_call | solution.py:293
  35.8 0.8 %shard_map.67 = (f32[64,512]{1,0:T(8,128)}, f32[64,512]{1,0:T(8,128)}, f32[67,268]{1,0:T(8,128)}, f32[64,268]{1,0:T(8,128)}) custom-call(f32[64,512]{1,0:T(8,128)S(1)} %get-tuple-element.12.red, f32[64,512]{1,0:T(8,128)S(1)} %get-tuple-element.13.rate, f32[67,268]{1,0:T(8,128)S(1)} %get-tuple-element.14.norm, f32[64,268]{1,0:T(8,128)S(1)} %get-tuple-element.15.rhs), custom_call_target="tpu_custom_call" | custom-call | tf_op jit(solution)/shard_map/pallas_call | solution.py:326

commit v3 on v2

v3 whole, which is shorter than its diff:
```python
import functools

import jax
import jax.numpy as jnp
from jax import lax
from jax.experimental import pallas as pl
from jax.experimental.pallas import tpu as pltpu
from jax.sharding import PartitionSpec as P

MESH = pl.DeviceIdType.MESH
F32 = jnp.float32
BF16 = jnp.bfloat16
CONTRACT = (((1,), (1,)), ((), ()))

NX, NY, NZ = 4, 4, 8
R = 64
FEATURES = 2144
SNAPS = 4096
GROUP = 512
LANES = 128
HALF = 256
ROWS = FEATURES // 8
COLS = FEATURES // 32
ROWS_P = 272
COLS_8 = 72
COLS_P = 2 * COLS_8
WIDE = 384
SEL = ROWS_P + COLS_P
XY_ORDER = [(dx, dy) for dx in (0, 1, 3, 2) for dy in (0, 1, 3, 2) if dx or dy]
Z_ORDER = (1, 7, 2, 6, 3, 5, 4)


def start_of(q):
    return R + R * q - (q * (q - 1)) // 2


def position():
    t, s = lax.axis_index("tm"), lax.axis_index("space")
    x, yh = t // 2, t % 2
    yl, z, c = s // 16, (s % 16) // 2, s % 2
    return t, s, x, yh * 2 + yl, z, c


def device_at(x, y, z, c):
    return (x * 2 + y // 2, (y % 2) * 16 + z * 2 + c)


def selectors(t, s, sel_ref):
    shape = (SEL, 256)
    row = lax.broadcasted_iota(jnp.int32, shape, 0)
    lane = lax.broadcasted_iota(jnp.int32, shape, 1)
    column = row - ROWS_P
    column = jnp.where(column < COLS_8, column, column - COLS_8 + COLS)
    f = jnp.where(row < ROWS_P, ROWS * t + row, 2 * COLS * (s // 2) + column)
    q = lane % R
    part = lane < 3 * R
    begin = start_of(q)
    linear = f < R
    first = (f >= begin) & (f < start_of(q + 1))
    first = ((linear & (f == q)) | first) & part
    count = jnp.sum(jnp.where((f >= begin) & (lane < R), 1.0, 0.0), axis=1, keepdims=True)
    i = count.astype(jnp.int32) - 1
    j = f - start_of(i) + i
    second = (linear & (lane == 3 * R)) | (~linear & (q == j) & part)
    sel_ref[:SEL, :] = jnp.where(first, 1.0, 0.0).astype(BF16)
    sel_ref[SEL:, :] = jnp.where(second, 1.0, 0.0).astype(BF16)


def split3(r):
    high = r.astype(BF16)
    rest = r - high.astype(F32)
    middle = rest.astype(BF16)
    low = (rest - middle.astype(F32)).astype(BF16)
    ones = jnp.where(lax.broadcasted_iota(jnp.int32, r.shape, 0) == 0, 1.0, 0.0).astype(BF16)
    return jnp.concatenate([high, middle, low, ones], axis=0)


def slopes(r):
    width = r.shape[1]
    return (pltpu.roll(r, width - 1, 1) - pltpu.roll(r, 1, 1)) * 0.5


def kernel(
    snap_hbm, basis_hbm, reg_hbm,
    red_ref, rate_ref, norm_ref, rhs_ref,
    snap_v, basis_v, reg_s, xbuf, ybuf, pbuf, rbuf, gbuf, sel, edge, oedge, acc, oacc,
    in_sem, rs_send, rs_recv, g1_send, g1_recv, g2_send, g2_recv, x_send, x_recv,
):
    t, s, x, y, z, c = position()
    yl = y % 2
    me = 4 * x + y
    other = device_at(x, y, z, 1 - c)

    basis_in = pltpu.make_async_copy(basis_hbm, basis_v, in_sem.at[2])
    basis_in.start()
    snaps_in = []
    for h, core in enumerate((1 - c, c)):
        rows = pl.ds(pl.multiple_of(core * HALF, HALF), HALF)
        copy = pltpu.make_async_copy(snap_hbm.at[rows], snap_v.at[h], in_sem.at[h])
        copy.start()
        snaps_in.append(copy)
    reg_in = pltpu.make_async_copy(reg_hbm, reg_s, in_sem.at[3])
    reg_in.start()

    barrier = pltpu.get_barrier_semaphore()
    peers = [other]
    for d in range(1, 16):
        w = (s // 2 + d) % 16
        peers.append((t, 2 * w + c))
    for dx in range(1, NX):
        for dy in range(NY):
            peers.append(device_at((x + dx) % NX, (y + dy) % NY, z, c))
    for d in range(2):
        peers.append(device_at(x, (y // 2 * 2 + 2) % 4 + d, z, c))
    for peer in peers:
        pl.semaphore_signal(barrier, inc=1, device_id=peer, device_id_type=MESH)

    def across(src, dst, k):
        return pltpu.make_async_remote_copy(
            src_ref=src, dst_ref=dst, send_sem=x_send.at[k], recv_sem=x_recv.at[k],
            device_id=other, device_id_type=MESH,
        )

    def projected(h):
        snaps_in[h].wait()
        return lax.dot_general(basis_v[...], snap_v[h], CONTRACT, preferred_element_type=F32)

    basis_in.wait()
    part = projected(0)
    for h in range(2):
        xbuf[h] = part[:, h * LANES:(h + 1) * LANES]
    pl.semaphore_wait(barrier, len(peers))
    send_part = across(xbuf, ybuf, 0)
    send_part.start()
    part = projected(1)
    send_part.wait()
    mine = s // 2
    for h in range(2):
        pbuf[h] = part[:, h * LANES:(h + 1) * LANES] + ybuf[h]
        for d in (4, 3, 5, 2, 6, 1, 7, 0):
            zz = (z + d) % NZ
            to = h * NZ + zz
            copy = pltpu.make_async_remote_copy(
                src_ref=pbuf.at[h, pl.ds(pl.multiple_of(8 * zz, 8), 8)],
                dst_ref=rbuf.at[(mine - to + 16) % 16],
                send_sem=rs_send, recv_sem=rs_recv,
                device_id=(t, 2 * to + c), device_id_type=MESH,
            )
            if d == 0:
                pl.when(to != mine)(copy.start)
            else:
                copy.start()

    reg_in.wait()
    pltpu.make_async_remote_copy(
        src_ref=rbuf.at[pl.ds(1, 15)], dst_ref=rbuf.at[pl.ds(1, 15)],
        send_sem=rs_send, recv_sem=rs_recv, device_id=other, device_id_type=MESH,
    ).wait()
    zrows = pl.ds(pl.multiple_of(8 * z, 8), 8)
    total = pbuf[yl, zrows, :]
    for d in range(1, 16):
        total = total + rbuf[d]
    gbuf[me, zrows, :] = total

    def tile(zz):
        return gbuf.at[me, pl.ds(pl.multiple_of(8 * zz, 8), 8)]

    def along_z(d):
        return pltpu.make_async_remote_copy(
            src_ref=tile(z), dst_ref=tile(z), send_sem=g1_send, recv_sem=g1_recv.at[d],
            device_id=device_at(x, y, (z + d) % NZ, c), device_id_type=MESH,
        )

    def over_xy(zz):
        for dx, dy in XY_ORDER:
            pltpu.make_async_remote_copy(
                src_ref=tile(zz), dst_ref=tile(zz), send_sem=g2_send, recv_sem=g2_recv.at[4 * dx + dy],
                device_id=device_at((x + dx) % NX, (y + dy) % NY, z, c), device_id_type=MESH,
            ).start()

    for d in Z_ORDER:
        along_z(d).start()
    over_xy(z)
    for d in Z_ORDER:
        along_z(d).wait_recv()
        over_xy((z - d + NZ) % NZ)

    own = pl.ds(pl.multiple_of(c * HALF, HALF), HALF)
    send_red = across(red_ref.at[:, own], red_ref.at[:, own], 4)
    selectors(t, s, sel)
    acc[...] = jnp.zeros_like(acc)
    edge[...] = jnp.zeros_like(edge)
    edge_lane = lax.broadcasted_iota(jnp.int32, (R, LANES), 1)
    wide_lane = lax.broadcasted_iota(jnp.int32, (R, 2 * HALF), 1) % HALF
    inside = (wide_lane != 0) & (wide_lane != HALF - 1)

    def products(k, carry):
        dx = k + k // 2 - 2 * (k // 3)
        xx = (x - dx + NX) % NX
        for yy in range(NY):
            dy = (y - yy + NY) % NY
            source = 4 * xx + yy
            arrived = pltpu.make_async_remote_copy(
                src_ref=gbuf.at[source], dst_ref=gbuf.at[source], send_sem=g2_send, recv_sem=g2_recv.at[4 * dx + dy],
                device_id=other, device_id_type=MESH,
            )
            pl.when(source != me)(arrived.wait_recv)
        blocks = [gbuf[4 * xx + yy] for yy in range(NY)]

        @pl.when(k == 0)
        def _():
            red_ref[:, own] = jnp.concatenate([gbuf[2 * t], gbuf[2 * t + 1]], axis=1)
            send_red.start()

        ends = edge[...]
        for h in range(2):
            spot = 4 * (2 * (2 * xx + h) + c)
            ends = jnp.where(edge_lane // 2 == spot // 2, pltpu.roll(blocks[2 * h], spot, 1), ends)
            ends = jnp.where(edge_lane // 2 == spot // 2 + 1, pltpu.roll(blocks[2 * h + 1], spot + 4, 1), ends)
        edge[...] = ends
        pl.when(k == 3)(across(edge, oedge, 1).start)
        r = jnp.concatenate(blocks, axis=1)
        rates = jnp.where(inside, slopes(r), 0.0).astype(BF16)
        picked = jnp.dot(sel[...], split3(r), preferred_element_type=F32)
        feature = (picked[:SEL] * picked[SEL:]).astype(BF16)
        columns = jnp.concatenate([feature[ROWS_P:], rates], axis=0)
        acc[:, :ROWS_P] += lax.dot_general(columns, feature[:ROWS_P], CONTRACT, preferred_element_type=F32)
        return carry

    lax.fori_loop(0, 4, products, 0)
    theirs = pl.ds(pl.multiple_of((1 - c) * COLS_8, 8), COLS_8)
    send_norm = across(acc.at[theirs], oacc.at[pl.ds(0, COLS_8)], 2)
    send_norm.start()
    send_rhs = across(acc.at[pl.ds(COLS_P, R)], oacc.at[pl.ds(COLS_8, R)], 3)
    send_rhs.start()
    pltpu.make_async_remote_copy(
        src_ref=gbuf.at[me, pl.ds(0, 56)], dst_ref=gbuf.at[me, pl.ds(0, 56)],
        send_sem=g1_send, recv_sem=g1_recv.at[0], device_id=other, device_id_type=MESH,
    ).wait_send()
    pltpu.make_async_remote_copy(
        src_ref=gbuf.at[pl.ds(0, 15)], dst_ref=gbuf.at[pl.ds(0, 15)],
        send_sem=g2_send, recv_sem=g1_recv.at[0], device_id=other, device_id_type=MESH,
    ).wait_send()
    across(edge, oedge, 1).wait()

    ends = jnp.where(edge_lane // 4 % 2 == c, edge[...], oedge[...])
    before, after = pltpu.roll(ends, 1, 1), pltpu.roll(ends, LANES - 1, 1)
    rate = (after - before) * 0.5
    rate = jnp.where(edge_lane == 0, after - ends, rate)
    rate = jnp.where(edge_lane == 63, ends - before, rate)
    at_end = (edge_lane < 64) & ((edge_lane % 4 == 0) | (edge_lane % 4 == 3))
    rate = jnp.where(at_end, rate, 0.0)
    parts = split3(ends)
    feature = jnp.dot(sel[:ROWS_P], parts, preferred_element_type=F32)
    feature = feature * jnp.dot(sel[SEL:SEL + ROWS_P], parts, preferred_element_type=F32)
    rest = lax.dot_general(rate.astype(BF16), feature.astype(BF16), CONTRACT, preferred_element_type=F32)

    send_red.wait()
    wide_lane = lax.broadcasted_iota(jnp.int32, (R, GROUP), 1)
    rates = slopes(red_ref[...])
    first = pltpu.roll(rate, (LANES - 8 * t) % LANES, 1)
    last = pltpu.roll(rate, LANES - 1 - (8 * t + 7), 1)
    pad = jnp.zeros((R, GROUP - LANES), F32)
    rates = jnp.where(wide_lane == 0, jnp.concatenate([first, pad], axis=1), rates)
    rate_ref[...] = jnp.where(wide_lane == GROUP - 1, jnp.concatenate([pad, last], axis=1), rates)

    spot = COLS * (s % 4)
    lane = lax.broadcasted_iota(jnp.int32, (8, WIDE), 1)

    def pick_weight(i, v):
        return jnp.where(lane == spot + i, reg_s[COLS * s + i], v)

    weight = lax.fori_loop(0, COLS, pick_weight, jnp.zeros((8, WIDE), F32))
    column = lax.broadcasted_iota(jnp.int32, (COLS, ROWS), 0)
    row = lax.broadcasted_iota(jnp.int32, (COLS, ROWS), 1)
    diagonal = (ROWS * t + row) == (COLS * s + column)
    send_norm.wait()
    summed = (acc[pl.ds(pl.multiple_of(c * COLS_8, 8), COLS_8), :] + oacc[:COLS_8, :]) * (1.0 / SNAPS)
    norm_ref[...] = summed[:COLS, :ROWS] + jnp.where(diagonal, weight[0:1, :ROWS], 0.0)
    send_rhs.wait()
    summed = acc[COLS_P:, :ROWS_P] + oacc[COLS_8:, :ROWS_P] + rest
    rhs_ref[...] = summed[:, :ROWS] * (1.0 / SNAPS)


def write(red, rate, norm, rhs, red_out, rate_out, norm_out, rhs_out, sem):
    pairs = ((red, red_out), (rate, rate_out), (norm, norm_out), (rhs, rhs_out))
    copies = [pltpu.make_async_copy(a, b, sem.at[k]) for k, (a, b) in enumerate(pairs)]
    for copy in copies:
        copy.start()
    for copy in copies:
        copy.wait()


def local(snapshots, modes_basis, reg_weights):
    f32 = lambda *shape: pltpu.VMEM(shape, F32)
    bf16 = lambda *shape: pltpu.VMEM(shape, BF16)
    dma = pltpu.SemaphoreType.DMA
    shapes = ((R, GROUP), (R, GROUP), (COLS, ROWS), (R, ROWS))
    in_hbm = lambda a: pltpu.with_memory_space_constraint(a, pltpu.HBM)
    in_vmem = lambda a: pltpu.with_memory_space_constraint(a, pltpu.VMEM)
    outs = pl.pallas_call(
        kernel,
        out_shape=tuple(f32(*shape) for shape in shapes),
        in_specs=[pl.BlockSpec(memory_space=pltpu.HBM)] * 3,
        out_specs=[pl.BlockSpec(memory_space=pltpu.VMEM)] * 4,
        scratch_shapes=[
            bf16(2, HALF, 2048),
            bf16(R, 2048),
            pltpu.SMEM((FEATURES,), F32),
            f32(2, R, LANES),
            f32(2, R, LANES),
            f32(2, R, LANES),
            f32(16, 8, LANES),
            f32(16, R, LANES),
            bf16(2 * SEL, 256),
            f32(R, LANES),
            f32(R, LANES),
            f32(COLS_P + R, WIDE),
            f32(COLS_8 + R, WIDE),
            dma((4,)),
            dma, dma,
            dma, dma((NZ,)),
            dma, dma((16,)),
            dma((5,)), dma((5,)),
        ],
        compiler_params=pltpu.CompilerParams(
            collective_id=0, has_side_effects=True, vmem_limit_bytes=32 * 1024 * 1024
        ),
        cost_estimate=pl.CostEstimate(flops=1 << 30, bytes_accessed=3 << 20, transcendentals=0),
    )(in_hbm(snapshots), in_hbm(modes_basis.T), in_hbm(reg_weights))
    outs = pl.pallas_call(
        write,
        out_shape=tuple(jax.ShapeDtypeStruct(shape, F32) for shape in shapes),
        in_specs=[pl.BlockSpec(memory_space=pltpu.VMEM)] * 4,
        out_specs=[pl.BlockSpec(memory_space=pltpu.HBM)] * 4,
        scratch_shapes=[dma((4,))],
        compiler_params=pltpu.CompilerParams(vmem_limit_bytes=4 * 1024 * 1024),
    )(*[in_vmem(out) for out in outs])
    return tuple(out.T for out in outs)


def solution(mesh):
    return jax.shard_map(
        local,
        mesh=mesh,
        in_specs=(P("tm", "space"), P("space", None), P()),
        out_specs=(P("tm", None), P("tm", None), P("tm", "space"), P("tm", None)),
        check_vma=False,
    )
```

time: 36.7 us -> 34.1 us (0.929)
  Pallas kernels: 36 us -> 33.4 us
    pallas_call x1, Pallas kernels: 35.2 us -> 32.6 us  [local(): pl.pallas_call(kernel, out_shape=tuple((f32(*shape) for shape in shapes))...]
where the time goes in v3:
time: 34.1 us; the launch traced here: 34 us
  Pallas kernels  33.4 us (98%)
  between operations  0.64 us (2%)
    pallas_call x1, Pallas kernels, local(): pl.pallas_call(kernel, out_shape=tuple((f32(*shape) for shape in shapes))...  32.6 us
    pallas_call x1, Pallas kernels, local(): pl.pallas_call(write, out_shape=tuple((jax.ShapeDtypeStruct(shape, F32) f...  0.8 us

profile of v3, /device:TPU:1, one launch (start us, length us, event | category | flops | bytes accessed | tf_op | source)
XLA Modules:
  0.0 34.0 jit_solution(7335177538574441121)
XLA Ops:
  0.6 32.6 %shard_map.66 = (f32[64,512]{1,0:T(8,128)S(1)}, f32[64,512]{1,0:T(8,128)S(1)}, f32[67,268]{1,0:T(8,128)S(1)}, f32[64,268]{1,0:T(8,128)S(1)}) custom-call(bf16[512,2048]{1,0:T(8,128)(2,1)} %snap_hbm.1, bf16[64,2048]{1,0:T(8,128)(2,1)} %bitcast.5, f32[2144]{0:T(1024)} %reg_hbm.1), custom_call_target="tpu_custom_call" | custom-call | flops 1073741824 | bytes 3145728 | tf_op jit(solution)/shard_map/pallas_call | solution.py:301
  33.2 0.8 %shard_map.67 = (f32[64,512]{1,0:T(8,128)}, f32[64,512]{1,0:T(8,128)}, f32[67,268]{1,0:T(8,128)}, f32[64,268]{1,0:T(8,128)}) custom-call(f32[64,512]{1,0:T(8,128)S(1)} %get-tuple-element.12.red, f32[64,512]{1,0:T(8,128)S(1)} %get-tuple-element.13.rate, f32[67,268]{1,0:T(8,128)S(1)} %get-tuple-element.14.norm, f32[64,268]{1,0:T(8,128)S(1)} %get-tuple-element.15.rhs), custom_call_target="tpu_custom_call" | custom-call | tf_op jit(solution)/shard_map/pallas_call | solution.py:331

commit v4 on v3

--- a/solution.py
+++ b/solution.py
@@ -27,7 +27,9 @@
 WIDE = 384
 SEL = ROWS_P + COLS_P
 XY_ORDER = [(dx, dy) for dx in (0, 1, 3, 2) for dy in (0, 1, 3, 2) if dx or dy]
-Z_ORDER = (1, 7, 2, 6, 3, 5, 4)
+Z_ORDER = (0, 1, 2, 3, 7, 4, 6, 5)
+OWNERS = 2
+TILE = R // OWNERS
 
 
 def start_of(q):
@@ -84,36 +86,47 @@
     snap_hbm, basis_hbm, reg_hbm,
     red_ref, rate_ref, norm_ref, rhs_ref,
     snap_v, basis_v, reg_s, xbuf, ybuf, pbuf, rbuf, gbuf, sel, edge, oedge, acc, oacc,
-    in_sem, rs_send, rs_recv, g1_send, g1_recv, g2_send, g2_recv, x_send, x_recv,
+    in_sem, rs_send, rs_recv, g1_send, g1_recv, g2_send, g2_recv, x_send, x_recv, go,
 ):
     t, s, x, y, z, c = position()
     yl = y % 2
     me = 4 * x + y
     other = device_at(x, y, z, 1 - c)
-
-    basis_in = pltpu.make_async_copy(basis_hbm, basis_v, in_sem.at[2])
+    partner = y // 2 * 2 + 1 - yl
+
+    basis_in = pltpu.make_async_copy(basis_hbm, basis_v, in_sem.at[4])
     basis_in.start()
     snaps_in = []
-    for h, core in enumerate((1 - c, c)):
-        rows = pl.ds(pl.multiple_of(core * HALF, HALF), HALF)
-        copy = pltpu.make_async_copy(snap_hbm.at[rows], snap_v.at[h], in_sem.at[h])
+    for k in range(4):
+        core = c if k >= 2 else 1 - c
+        rows = pl.ds(pl.multiple_of(core * HALF + k % 2 * LANES, LANES), LANES)
+        copy = pltpu.make_async_copy(snap_hbm.at[rows], snap_v.at[k], in_sem.at[k])
         copy.start()
         snaps_in.append(copy)
-    reg_in = pltpu.make_async_copy(reg_hbm, reg_s, in_sem.at[3])
+    reg_in = pltpu.make_async_copy(reg_hbm, reg_s, in_sem.at[5])
     reg_in.start()
 
     barrier = pltpu.get_barrier_semaphore()
-    peers = [other]
-    for d in range(1, 16):
-        w = (s // 2 + d) % 16
-        peers.append((t, 2 * w + c))
-    for dx in range(1, NX):
-        for dy in range(NY):
-            peers.append(device_at((x + dx) % NX, (y + dy) % NY, z, c))
-    for d in range(2):
-        peers.append(device_at(x, (y // 2 * 2 + 2) % 4 + d, z, c))
-    for peer in peers:
-        pl.semaphore_signal(barrier, inc=1, device_id=peer, device_id_type=MESH)
+
+    def greet(chip, core):
+        pl.semaphore_signal(barrier, inc=1, device_id=device_at(*chip, core), device_id_type=MESH)
+
+    pl.when(c == 1)(lambda: greet((x, y, z), 0))
+
+    @pl.when(z < OWNERS)
+    def _():
+        for d in range(1, NZ):
+            for yy in (partner, y):
+                greet((x, yy, (z + d) % NZ), 0)
+        greet((x, partner, z), 0)
+
+    for dx, dy in XY_ORDER:
+        greet(((x + dx) % NX, (y + dy) % NY, z), 1)
+
+    @pl.when(c == 0)
+    def _():
+        pl.semaphore_wait(barrier, 1 + 2 * (2 * OWNERS - 1) + 2 * (z // OWNERS > 0).astype(jnp.int32))
+        pl.semaphore_signal(go, inc=1, device_id=other, device_id_type=MESH)
 
     def across(src, dst, k):
         return pltpu.make_async_remote_copy(
@@ -121,55 +134,41 @@
             device_id=other, device_id_type=MESH,
         )
 
-    def projected(h):
-        snaps_in[h].wait()
-        return lax.dot_general(basis_v[...], snap_v[h], CONTRACT, preferred_element_type=F32)
+    def projected(k):
+        snaps_in[k].wait()
+        return lax.dot_general(basis_v[...], snap_v[k], CONTRACT, preferred_element_type=F32)
 
     basis_in.wait()
-    part = projected(0)
     for h in range(2):
-        xbuf[h] = part[:, h * LANES:(h + 1) * LANES]
-    pl.semaphore_wait(barrier, len(peers))
+        xbuf[h] = projected(h)
+    pl.when(c == 1)(lambda: pl.semaphore_wait(go, 1))
     send_part = across(xbuf, ybuf, 0)
     send_part.start()
-    part = projected(1)
-    send_part.wait()
+    for h in range(2):
+        pbuf[h] = projected(2 + h)
+    send_part.wait_recv()
     mine = s // 2
     for h in range(2):
-        pbuf[h] = part[:, h * LANES:(h + 1) * LANES] + ybuf[h]
-        for d in (4, 3, 5, 2, 6, 1, 7, 0):
-            zz = (z + d) % NZ
+        pbuf[h] += ybuf[h]
+        for zz in range(OWNERS):
             to = h * NZ + zz
             copy = pltpu.make_async_remote_copy(
-                src_ref=pbuf.at[h, pl.ds(pl.multiple_of(8 * zz, 8), 8)],
-                dst_ref=rbuf.at[(mine - to + 16) % 16],
+                src_ref=pbuf.at[h, pl.ds(TILE * zz, TILE)], dst_ref=rbuf.at[(mine - to + 16) % 16],
                 send_sem=rs_send, recv_sem=rs_recv,
                 device_id=(t, 2 * to + c), device_id_type=MESH,
             )
-            if d == 0:
-                pl.when(to != mine)(copy.start)
-            else:
-                copy.start()
+            pl.when(to != mine)(copy.start)
 
     reg_in.wait()
-    pltpu.make_async_remote_copy(
-        src_ref=rbuf.at[pl.ds(1, 15)], dst_ref=rbuf.at[pl.ds(1, 15)],
-        send_sem=rs_send, recv_sem=rs_recv, device_id=other, device_id_type=MESH,
-    ).wait()
-    zrows = pl.ds(pl.multiple_of(8 * z, 8), 8)
-    total = pbuf[yl, zrows, :]
-    for d in range(1, 16):
-        total = total + rbuf[d]
-    gbuf[me, zrows, :] = total
+    @pl.when(c == 1)
+    def _():
+        pl.semaphore_wait(barrier, 2 * (NX * NY - 1))
+        pl.semaphore_signal(go, inc=1, device_id=other, device_id_type=MESH)
+
+    pl.when(c == 0)(lambda: pl.semaphore_wait(go, 1))
 
     def tile(zz):
-        return gbuf.at[me, pl.ds(pl.multiple_of(8 * zz, 8), 8)]
-
-    def along_z(d):
-        return pltpu.make_async_remote_copy(
-            src_ref=tile(z), dst_ref=tile(z), send_sem=g1_send, recv_sem=g1_recv.at[d],
-            device_id=device_at(x, y, (z + d) % NZ, c), device_id_type=MESH,
-        )
+        return gbuf.at[me, pl.ds(pl.multiple_of(TILE * zz, TILE), TILE)]
 
     def over_xy(zz):
         for dx, dy in XY_ORDER:
@@ -178,12 +177,35 @@
                 device_id=device_at((x + dx) % NX, (y + dy) % NY, z, c), device_id_type=MESH,
             ).start()
 
-    for d in Z_ORDER:
-        along_z(d).start()
-    over_xy(z)
-    for d in Z_ORDER:
-        along_z(d).wait_recv()
-        over_xy((z - d + NZ) % NZ)
+    @pl.when(z < OWNERS)
+    def _():
+        pltpu.make_async_remote_copy(
+            src_ref=rbuf.at[pl.ds(1, 15)], dst_ref=rbuf.at[pl.ds(1, 15)],
+            send_sem=rs_send, recv_sem=rs_recv, device_id=other, device_id_type=MESH,
+        ).wait_recv()
+        rows = pl.ds(pl.multiple_of(TILE * z, TILE), TILE)
+        total = pbuf[yl, rows, :]
+        for d in range(1, 16):
+            total = total + rbuf[d]
+        gbuf[me, rows, :] = total
+        for zz in Z_ORDER:
+            copy = pltpu.make_async_remote_copy(
+                src_ref=tile(z), dst_ref=tile(z), send_sem=g1_send, recv_sem=g1_recv.at[z],
+                device_id=device_at(x, y, zz, c), device_id_type=MESH,
+            )
+            pl.when(zz != z)(copy.start)
+        over_xy(z)
+
+    for k in range(OWNERS):
+        zz = jnp.where(z < OWNERS, z + k, jnp.where(z < 6, OWNERS - 1 - k, k)) % OWNERS
+
+        @pl.when(zz != z)
+        def _():
+            pltpu.make_async_remote_copy(
+                src_ref=tile(zz), dst_ref=tile(zz), send_sem=g1_send, recv_sem=g1_recv.at[zz],
+                device_id=other, device_id_type=MESH,
+            ).wait_recv()
+            over_xy(zz)
 
     own = pl.ds(pl.multiple_of(c * HALF, HALF), HALF)
     send_red = across(red_ref.at[:, own], red_ref.at[:, own], 4)
@@ -233,15 +255,8 @@
     send_norm.start()
     send_rhs = across(acc.at[pl.ds(COLS_P, R)], oacc.at[pl.ds(COLS_8, R)], 3)
     send_rhs.start()
-    pltpu.make_async_remote_copy(
-        src_ref=gbuf.at[me, pl.ds(0, 56)], dst_ref=gbuf.at[me, pl.ds(0, 56)],
-        send_sem=g1_send, recv_sem=g1_recv.at[0], device_id=other, device_id_type=MESH,
-    ).wait_send()
-    pltpu.make_async_remote_copy(
-        src_ref=gbuf.at[pl.ds(0, 15)], dst_ref=gbuf.at[pl.ds(0, 15)],
-        send_sem=g2_send, recv_sem=g1_recv.at[0], device_id=other, device_id_type=MESH,
-    ).wait_send()
-    across(edge, oedge, 1).wait()
+    send_edge = across(edge, oedge, 1)
+    send_edge.wait_recv()
 
     ends = jnp.where(edge_lane // 4 % 2 == c, edge[...], oedge[...])
     before, after = pltpu.roll(ends, 1, 1), pltpu.roll(ends, LANES - 1, 1)
@@ -255,7 +270,7 @@
     feature = feature * jnp.dot(sel[SEL:SEL + ROWS_P], parts, preferred_element_type=F32)
     rest = lax.dot_general(rate.astype(BF16), feature.astype(BF16), CONTRACT, preferred_element_type=F32)
 
-    send_red.wait()
+    send_red.wait_recv()
     wide_lane = lax.broadcasted_iota(jnp.int32, (R, GROUP), 1)
     rates = slopes(red_ref[...])
     first = pltpu.roll(rate, (LANES - 8 * t) % LANES, 1)
@@ -274,12 +289,25 @@
     column = lax.broadcasted_iota(jnp.int32, (COLS, ROWS), 0)
     row = lax.broadcasted_iota(jnp.int32, (COLS, ROWS), 1)
     diagonal = (ROWS * t + row) == (COLS * s + column)
-    send_norm.wait()
+    send_norm.wait_recv()
     summed = (acc[pl.ds(pl.multiple_of(c * COLS_8, 8), COLS_8), :] + oacc[:COLS_8, :]) * (1.0 / SNAPS)
     norm_ref[...] = summed[:COLS, :ROWS] + jnp.where(diagonal, weight[0:1, :ROWS], 0.0)
-    send_rhs.wait()
+    send_rhs.wait_recv()
     summed = acc[COLS_P:, :ROWS_P] + oacc[COLS_8:, :ROWS_P] + rest
     rhs_ref[...] = summed[:, :ROWS] * (1.0 / SNAPS)
+
+
+    def sent(ref, sem):
+        pltpu.make_async_remote_copy(
+            src_ref=ref, dst_ref=ref, send_sem=sem, recv_sem=g1_recv.at[0], device_id=other, device_id_type=MESH,
+        ).wait_send()
+
+    sent(gbuf.at[pl.ds(0, 15)], g2_send)
+    sent(rbuf.at[pl.ds(0, 2 * OWNERS - 1)], rs_send)
+    pl.when(z >= OWNERS)(lambda: sent(rbuf.at[0], rs_send))
+    pl.when(z < OWNERS)(lambda: sent(rbuf.at[pl.ds(0, 7)], g1_send))
+    for copy in (send_part, send_edge, send_red, send_norm, send_rhs):
+        copy.wait_send()
 
 
 def write(red, rate, norm, rhs, red_out, rate_out, norm_out, rhs_out, sem):
@@ -304,24 +332,25 @@
         in_specs=[pl.BlockSpec(memory_space=pltpu.HBM)] * 3,
         out_specs=[pl.BlockSpec(memory_space=pltpu.VMEM)] * 4,
         scratch_shapes=[
-            bf16(2, HALF, 2048),
+            bf16(4, LANES, 2048),
             bf16(R, 2048),
             pltpu.SMEM((FEATURES,), F32),
             f32(2, R, LANES),
             f32(2, R, LANES),
             f32(2, R, LANES),
-            f32(16, 8, LANES),
+            f32(16, TILE, LANES),
             f32(16, R, LANES),
             bf16(2 * SEL, 256),
             f32(R, LANES),
             f32(R, LANES),
             f32(COLS_P + R, WIDE),
             f32(COLS_8 + R, WIDE),
-            dma((4,)),
+            dma((6,)),
             dma, dma,
-            dma, dma((NZ,)),
+            dma, dma((OWNERS,)),
             dma, dma((16,)),
             dma((5,)), dma((5,)),
+            pltpu.SemaphoreType.REGULAR,
         ],
         compiler_params=pltpu.CompilerParams(
             collective_id=0, has_side_effects=True, vmem_limit_bytes=32 * 1024 * 1024

time: 34.1 us -> 32.3 us (0.947)
  Pallas kernels: 33.4 us -> 31.5 us
    pallas_call x1, Pallas kernels: 32.6 us -> 30.7 us  [local(): pl.pallas_call(kernel, out_shape=tuple((f32(*shape) for shape in shapes))...]
where the time goes in v4:
time: 32.3 us; the launch traced here: 32.2 us
  Pallas kernels  31.5 us (98%)
  between operations  0.64 us (2%)
    pallas_call x1, Pallas kernels, local(): pl.pallas_call(kernel, out_shape=tuple((f32(*shape) for shape in shapes))...  30.7 us
    pallas_call x1, Pallas kernels, local(): pl.pallas_call(write, out_shape=tuple((jax.ShapeDtypeStruct(shape, F32) f...  0.8 us

profile of v4, /device:TPU:1, one launch (start us, length us, event | category | flops | bytes accessed | tf_op | source)
XLA Modules:
  0.0 32.2 jit_solution(12593708841363491621)
XLA Ops:
  0.6 30.7 %shard_map.66 = (f32[64,512]{1,0:T(8,128)S(1)}, f32[64,512]{1,0:T(8,128)S(1)}, f32[67,268]{1,0:T(8,128)S(1)}, f32[64,268]{1,0:T(8,128)S(1)}) custom-call(bf16[512,2048]{1,0:T(8,128)(2,1)} %snap_hbm.1, bf16[64,2048]{1,0:T(8,128)(2,1)} %bitcast.5, f32[2144]{0:T(1024)} %reg_hbm.1), custom_call_target="tpu_custom_call" | custom-call | flops 1073741824 | bytes 3145728 | tf_op jit(solution)/shard_map/pallas_call | solution.py:329
  31.4 0.8 %shard_map.67 = (f32[64,512]{1,0:T(8,128)}, f32[64,512]{1,0:T(8,128)}, f32[67,268]{1,0:T(8,128)}, f32[64,268]{1,0:T(8,128)}) custom-call(f32[64,512]{1,0:T(8,128)S(1)} %get-tuple-element.12.red, f32[64,512]{1,0:T(8,128)S(1)} %get-tuple-element.13.rate, f32[67,268]{1,0:T(8,128)S(1)} %get-tuple-element.14.norm, f32[64,268]{1,0:T(8,128)S(1)} %get-tuple-element.15.rhs), custom_call_target="tpu_custom_call" | custom-call | tf_op jit(solution)/shard_map/pallas_call | solution.py:360

commit v5 on v4

--- a/solution.py
+++ b/solution.py
@@ -29,6 +29,7 @@
 XY_ORDER = [(dx, dy) for dx in (0, 1, 3, 2) for dy in (0, 1, 3, 2) if dx or dy]
 Z_ORDER = (0, 1, 2, 3, 7, 4, 6, 5)
 OWNERS = 2
+STRIDE = 3
 TILE = R // OWNERS
 
 
@@ -68,6 +69,16 @@
     sel_ref[SEL:, :] = jnp.where(second, 1.0, 0.0).astype(BF16)
 
 
+def weights(s, reg_s):
+    spot = COLS * (s % 4)
+    lane = lax.broadcasted_iota(jnp.int32, (8, WIDE), 1)
+
+    def pick(i, v):
+        return jnp.where(lane == spot + i, reg_s[COLS * s + i], v)
+
+    return lax.fori_loop(0, COLS, pick, jnp.zeros((8, WIDE), F32))
+
+
 def split3(r):
     high = r.astype(BF16)
     rest = r - high.astype(F32)
@@ -91,6 +102,8 @@
     t, s, x, y, z, c = position()
     yl = y % 2
     me = 4 * x + y
+    nth = z // STRIDE
+    owns = (z % STRIDE == 0) & (nth < OWNERS)
     other = device_at(x, y, z, 1 - c)
     partner = y // 2 * 2 + 1 - yl
 
@@ -113,7 +126,7 @@
 
     pl.when(c == 1)(lambda: greet((x, y, z), 0))
 
-    @pl.when(z < OWNERS)
+    @pl.when(owns)
     def _():
         for d in range(1, NZ):
             for yy in (partner, y):
@@ -125,7 +138,7 @@
 
     @pl.when(c == 0)
     def _():
-        pl.semaphore_wait(barrier, 1 + 2 * (2 * OWNERS - 1) + 2 * (z // OWNERS > 0).astype(jnp.int32))
+        pl.semaphore_wait(barrier, 1 + 2 * (2 * OWNERS - 1) + 2 * (1 - owns.astype(jnp.int32)))
         pl.semaphore_signal(go, inc=1, device_id=other, device_id_type=MESH)
 
     def across(src, dst, k):
@@ -139,19 +152,19 @@
         return lax.dot_general(basis_v[...], snap_v[k], CONTRACT, preferred_element_type=F32)
 
     basis_in.wait()
-    for h in range(2):
-        xbuf[h] = projected(h)
+    xbuf[0] = projected(0)
     pl.when(c == 1)(lambda: pl.semaphore_wait(go, 1))
-    send_part = across(xbuf, ybuf, 0)
-    send_part.start()
-    for h in range(2):
-        pbuf[h] = projected(2 + h)
-    send_part.wait_recv()
+    send_parts = [across(xbuf.at[h], ybuf.at[h], 5 * h) for h in range(2)]
+    send_parts[0].start()
+    xbuf[1] = projected(1)
+    send_parts[1].start()
     mine = s // 2
     for h in range(2):
-        pbuf[h] += ybuf[h]
+        part = projected(2 + h)
+        send_parts[h].wait_recv()
+        pbuf[h] = part + ybuf[h]
         for zz in range(OWNERS):
-            to = h * NZ + zz
+            to = h * NZ + STRIDE * zz
             copy = pltpu.make_async_remote_copy(
                 src_ref=pbuf.at[h, pl.ds(TILE * zz, TILE)], dst_ref=rbuf.at[(mine - to + 16) % 16],
                 send_sem=rs_send, recv_sem=rs_recv,
@@ -160,6 +173,11 @@
             pl.when(to != mine)(copy.start)
 
     reg_in.wait()
+    selectors(t, s, sel)
+    acc[...] = jnp.zeros_like(acc)
+    edge[...] = jnp.zeros_like(edge)
+    weight = weights(s, reg_s)
+
     @pl.when(c == 1)
     def _():
         pl.semaphore_wait(barrier, 2 * (NX * NY - 1))
@@ -177,29 +195,29 @@
                 device_id=device_at((x + dx) % NX, (y + dy) % NY, z, c), device_id_type=MESH,
             ).start()
 
-    @pl.when(z < OWNERS)
+    @pl.when(owns)
     def _():
         pltpu.make_async_remote_copy(
             src_ref=rbuf.at[pl.ds(1, 15)], dst_ref=rbuf.at[pl.ds(1, 15)],
             send_sem=rs_send, recv_sem=rs_recv, device_id=other, device_id_type=MESH,
         ).wait_recv()
-        rows = pl.ds(pl.multiple_of(TILE * z, TILE), TILE)
+        rows = pl.ds(pl.multiple_of(TILE * nth, TILE), TILE)
         total = pbuf[yl, rows, :]
         for d in range(1, 16):
             total = total + rbuf[d]
         gbuf[me, rows, :] = total
         for zz in Z_ORDER:
             copy = pltpu.make_async_remote_copy(
-                src_ref=tile(z), dst_ref=tile(z), send_sem=g1_send, recv_sem=g1_recv.at[z],
+                src_ref=tile(nth), dst_ref=tile(nth), send_sem=g1_send, recv_sem=g1_recv.at[nth],
                 device_id=device_at(x, y, zz, c), device_id_type=MESH,
             )
             pl.when(zz != z)(copy.start)
-        over_xy(z)
+        over_xy(nth)
 
     for k in range(OWNERS):
-        zz = jnp.where(z < OWNERS, z + k, jnp.where(z < 6, OWNERS - 1 - k, k)) % OWNERS
-
-        @pl.when(zz != z)
+        zz = jnp.where(owns, nth + k, jnp.where((z > 1) & (z < 6), OWNERS - 1 - k, k)) % OWNERS
+
+        @pl.when(~(owns & (zz == nth)))
         def _():
             pltpu.make_async_remote_copy(
                 src_ref=tile(zz), dst_ref=tile(zz), send_sem=g1_send, recv_sem=g1_recv.at[zz],
@@ -209,9 +227,6 @@
 
     own = pl.ds(pl.multiple_of(c * HALF, HALF), HALF)
     send_red = across(red_ref.at[:, own], red_ref.at[:, own], 4)
-    selectors(t, s, sel)
-    acc[...] = jnp.zeros_like(acc)
-    edge[...] = jnp.zeros_like(edge)
     edge_lane = lax.broadcasted_iota(jnp.int32, (R, LANES), 1)
     wide_lane = lax.broadcasted_iota(jnp.int32, (R, 2 * HALF), 1) % HALF
     inside = (wide_lane != 0) & (wide_lane != HALF - 1)
@@ -279,13 +294,6 @@
     rates = jnp.where(wide_lane == 0, jnp.concatenate([first, pad], axis=1), rates)
     rate_ref[...] = jnp.where(wide_lane == GROUP - 1, jnp.concatenate([pad, last], axis=1), rates)
 
-    spot = COLS * (s % 4)
-    lane = lax.broadcasted_iota(jnp.int32, (8, WIDE), 1)
-
-    def pick_weight(i, v):
-        return jnp.where(lane == spot + i, reg_s[COLS * s + i], v)
-
-    weight = lax.fori_loop(0, COLS, pick_weight, jnp.zeros((8, WIDE), F32))
     column = lax.broadcasted_iota(jnp.int32, (COLS, ROWS), 0)
     row = lax.broadcasted_iota(jnp.int32, (COLS, ROWS), 1)
     diagonal = (ROWS * t + row) == (COLS * s + column)
@@ -304,9 +312,9 @@
 
     sent(gbuf.at[pl.ds(0, 15)], g2_send)
     sent(rbuf.at[pl.ds(0, 2 * OWNERS - 1)], rs_send)
-    pl.when(z >= OWNERS)(lambda: sent(rbuf.at[0], rs_send))
-    pl.when(z < OWNERS)(lambda: sent(rbuf.at[pl.ds(0, 7)], g1_send))
-    for copy in (send_part, send_edge, send_red, send_norm, send_rhs):
+    pl.when(~owns)(lambda: sent(rbuf.at[0], rs_send))
+    pl.when(owns)(lambda: sent(rbuf.at[pl.ds(0, 7)], g1_send))
+    for copy in (*send_parts, send_edge, send_red, send_norm, send_rhs):
         copy.wait_send()
 
 
@@ -349,7 +357,7 @@
             dma, dma,
             dma, dma((OWNERS,)),
             dma, dma((16,)),
-            dma((5,)), dma((5,)),
+            dma((6,)), dma((6,)),
             pltpu.SemaphoreType.REGULAR,
         ],
         compiler_params=pltpu.CompilerParams(

time: 32.3 us -> 31.8 us (0.985)
  Pallas kernels: 31.5 us -> 31 us
    pallas_call x1, Pallas kernels: 30.7 us -> 30.2 us  [local(): pl.pallas_call(kernel, out_shape=tuple((f32(*shape) for shape in shapes))...]
where the time goes in v5:
time: 31.8 us; the launch traced here: 31.7 us
  Pallas kernels  31 us (97%)
  between operations  0.64 us (2%)
    pallas_call x1, Pallas kernels, local(): pl.pallas_call(kernel, out_shape=tuple((f32(*shape) for shape in shapes))...  30.2 us
    pallas_call x1, Pallas kernels, local(): pl.pallas_call(write, out_shape=tuple((jax.ShapeDtypeStruct(shape, F32) f...  0.8 us

profile of v5, /device:TPU:1, one launch (start us, length us, event | category | flops | bytes accessed | tf_op | source)
XLA Modules:
  0.0 31.7 jit_solution(7423814858328844743)
XLA Ops:
  0.6 30.2 %shard_map.66 = (f32[64,512]{1,0:T(8,128)S(1)}, f32[64,512]{1,0:T(8,128)S(1)}, f32[67,268]{1,0:T(8,128)S(1)}, f32[64,268]{1,0:T(8,128)S(1)}) custom-call(bf16[512,2048]{1,0:T(8,128)(2,1)} %snap_hbm.1, bf16[64,2048]{1,0:T(8,128)(2,1)} %bitcast.5, f32[2144]{0:T(1024)} %reg_hbm.1), custom_call_target="tpu_custom_call" | custom-call | flops 1073741824 | bytes 3145728 | tf_op jit(solution)/shard_map/pallas_call | solution.py:337
  30.9 0.8 %shard_map.67 = (f32[64,512]{1,0:T(8,128)}, f32[64,512]{1,0:T(8,128)}, f32[67,268]{1,0:T(8,128)}, f32[64,268]{1,0:T(8,128)}) custom-call(f32[64,512]{1,0:T(8,128)S(1)} %get-tuple-element.12.red, f32[64,512]{1,0:T(8,128)S(1)} %get-tuple-element.13.rate, f32[67,268]{1,0:T(8,128)S(1)} %get-tuple-element.14.norm, f32[64,268]{1,0:T(8,128)S(1)} %get-tuple-element.15.rhs), custom_call_target="tpu_custom_call" | custom-call | tf_op jit(solution)/shard_map/pallas_call | solution.py:368

commit v6 on v5

--- a/solution.py
+++ b/solution.py
@@ -27,6 +27,7 @@
 WIDE = 384
 SEL = ROWS_P + COLS_P
 XY_ORDER = [(dx, dy) for dx in (0, 1, 3, 2) for dy in (0, 1, 3, 2) if dx or dy]
+XY_TARGETS = sorted(((x, y) for x in range(NX) for y in range(NY)), key=lambda p: (2 * p[0] + 3 * p[1], p))
 Z_ORDER = (0, 1, 2, 3, 7, 4, 6, 5)
 OWNERS = 2
 STRIDE = 3
@@ -37,15 +38,23 @@
     return R + R * q - (q * (q - 1)) // 2
 
 
+def over(a, b):
+    return lax.div(a, jnp.int32(b))
+
+
+def rest_of(a, b):
+    return lax.rem(a, jnp.int32(b))
+
+
 def position():
     t, s = lax.axis_index("tm"), lax.axis_index("space")
-    x, yh = t // 2, t % 2
-    yl, z, c = s // 16, (s % 16) // 2, s % 2
+    x, yh = over(t, 2), rest_of(t, 2)
+    yl, z, c = over(s, 16), over(rest_of(s, 16), 2), rest_of(s, 2)
     return t, s, x, yh * 2 + yl, z, c
 
 
 def device_at(x, y, z, c):
-    return (x * 2 + y // 2, (y % 2) * 16 + z * 2 + c)
+    return (x * 2 + over(y, 2), rest_of(y, 2) * 16 + z * 2 + c)
 
 
 def selectors(t, s, sel_ref):
@@ -100,12 +109,12 @@
     in_sem, rs_send, rs_recv, g1_send, g1_recv, g2_send, g2_recv, x_send, x_recv, go,
 ):
     t, s, x, y, z, c = position()
-    yl = y % 2
+    yl = rest_of(y, 2)
     me = 4 * x + y
-    nth = z // STRIDE
-    owns = (z % STRIDE == 0) & (nth < OWNERS)
+    nth = over(z, STRIDE)
+    owns = (rest_of(z, STRIDE) == 0) & (nth < OWNERS)
     other = device_at(x, y, z, 1 - c)
-    partner = y // 2 * 2 + 1 - yl
+    partner = y + 1 - 2 * yl
 
     basis_in = pltpu.make_async_copy(basis_hbm, basis_v, in_sem.at[4])
     basis_in.start()
@@ -130,11 +139,11 @@
     def _():
         for d in range(1, NZ):
             for yy in (partner, y):
-                greet((x, yy, (z + d) % NZ), 0)
+                greet((x, yy, rest_of(z + d, NZ)), 0)
         greet((x, partner, z), 0)
 
     for dx, dy in XY_ORDER:
-        greet(((x + dx) % NX, (y + dy) % NY, z), 1)
+        greet((rest_of(x + dx, NX), rest_of(y + dy, NY), z), 1)
 
     @pl.when(c == 0)
     def _():
@@ -158,7 +167,7 @@
     send_parts[0].start()
     xbuf[1] = projected(1)
     send_parts[1].start()
-    mine = s // 2
+    mine = over(s, 2)
     for h in range(2):
         part = projected(2 + h)
         send_parts[h].wait_recv()
@@ -166,7 +175,7 @@
         for zz in range(OWNERS):
             to = h * NZ + STRIDE * zz
             copy = pltpu.make_async_remote_copy(
-                src_ref=pbuf.at[h, pl.ds(TILE * zz, TILE)], dst_ref=rbuf.at[(mine - to + 16) % 16],
+                src_ref=pbuf.at[h, pl.ds(TILE * zz, TILE)], dst_ref=rbuf.at[rest_of(mine - to + 16, 16)],
                 send_sem=rs_send, recv_sem=rs_recv,
                 device_id=(t, 2 * to + c), device_id_type=MESH,
             )
@@ -189,11 +198,13 @@
         return gbuf.at[me, pl.ds(pl.multiple_of(TILE * zz, TILE), TILE)]
 
     def over_xy(zz):
-        for dx, dy in XY_ORDER:
-            pltpu.make_async_remote_copy(
-                src_ref=tile(zz), dst_ref=tile(zz), send_sem=g2_send, recv_sem=g2_recv.at[4 * dx + dy],
-                device_id=device_at((x + dx) % NX, (y + dy) % NY, z, c), device_id_type=MESH,
-            ).start()
+        held = tile(zz)
+        for xx, yy in XY_TARGETS:
+            copy = pltpu.make_async_remote_copy(
+                src_ref=held, dst_ref=held, send_sem=g2_send, recv_sem=g2_recv.at[me],
+                device_id=(2 * xx + yy // 2, 16 * (yy % 2) + 2 * z + c), device_id_type=MESH,
+            )
+            pl.when(me != 4 * xx + yy)(copy.start)
 
     @pl.when(owns)
     def _():
@@ -215,7 +226,7 @@
         over_xy(nth)
 
     for k in range(OWNERS):
-        zz = jnp.where(owns, nth + k, jnp.where((z > 1) & (z < 6), OWNERS - 1 - k, k)) % OWNERS
+        zz = rest_of(jnp.where(owns, nth + k, jnp.where((z > 1) & (z < 6), OWNERS - 1 - k, k)), OWNERS)
 
         @pl.when(~(owns & (zz == nth)))
         def _():
@@ -232,19 +243,17 @@
     inside = (wide_lane != 0) & (wide_lane != HALF - 1)
 
     def products(k, carry):
-        dx = k + k // 2 - 2 * (k // 3)
-        xx = (x - dx + NX) % NX
+        xx = k
         for yy in range(NY):
-            dy = (y - yy + NY) % NY
             source = 4 * xx + yy
             arrived = pltpu.make_async_remote_copy(
-                src_ref=gbuf.at[source], dst_ref=gbuf.at[source], send_sem=g2_send, recv_sem=g2_recv.at[4 * dx + dy],
+                src_ref=gbuf.at[source], dst_ref=gbuf.at[source], send_sem=g2_send, recv_sem=g2_recv.at[source],
                 device_id=other, device_id_type=MESH,
             )
             pl.when(source != me)(arrived.wait_recv)
         blocks = [gbuf[4 * xx + yy] for yy in range(NY)]
 
-        @pl.when(k == 0)
+        @pl.when(xx == x)
         def _():
             red_ref[:, own] = jnp.concatenate([gbuf[2 * t], gbuf[2 * t + 1]], axis=1)
             send_red.start()

time: 31.8 us -> 30.9 us (0.972); the launches traced: 31.7 us -> 30.4 us
  Pallas kernels: 31 us -> 29.7 us
    pallas_call x1, Pallas kernels: 30.2 us -> 28.9 us  [local(): pl.pallas_call(kernel, out_shape=tuple((f32(*shape) for shape in shapes))...]
where the time goes in v6:
time: 30.9 us; the launch traced here: 30.4 us
  Pallas kernels  29.7 us (96%)
  between operations  0.64 us (2%)
    pallas_call x1, Pallas kernels, local(): pl.pallas_call(kernel, out_shape=tuple((f32(*shape) for shape in shapes))...  28.9 us
    pallas_call x1, Pallas kernels, local(): pl.pallas_call(write, out_shape=tuple((jax.ShapeDtypeStruct(shape, F32) f...  0.8 us

profile of v6, /device:TPU:1, one launch (start us, length us, event | category | flops | bytes accessed | tf_op | source)
XLA Modules:
  0.0 30.4 jit_solution(18404639753592932217)
XLA Ops:
  0.6 28.9 %shard_map.66 = (f32[64,512]{1,0:T(8,128)S(1)}, f32[64,512]{1,0:T(8,128)S(1)}, f32[67,268]{1,0:T(8,128)S(1)}, f32[64,268]{1,0:T(8,128)S(1)}) custom-call(bf16[512,2048]{1,0:T(8,128)(2,1)} %snap_hbm.1, bf16[64,2048]{1,0:T(8,128)(2,1)} %bitcast.5, f32[2144]{0:T(1024)} %reg_hbm.1), custom_call_target="tpu_custom_call" | custom-call | flops 1073741824 | bytes 3145728 | tf_op jit(solution)/shard_map/pallas_call | solution.py:346
  29.6 0.8 %shard_map.67 = (f32[64,512]{1,0:T(8,128)}, f32[64,512]{1,0:T(8,128)}, f32[67,268]{1,0:T(8,128)}, f32[64,268]{1,0:T(8,128)}) custom-call(f32[64,512]{1,0:T(8,128)S(1)} %get-tuple-element.12.red, f32[64,512]{1,0:T(8,128)S(1)} %get-tuple-element.13.rate, f32[67,268]{1,0:T(8,128)S(1)} %get-tuple-element.14.norm, f32[64,268]{1,0:T(8,128)S(1)} %get-tuple-element.15.rhs), custom_call_target="tpu_custom_call" | custom-call | tf_op jit(solution)/shard_map/pallas_call | solution.py:377

commit v7 on v6

--- a/solution.py
+++ b/solution.py
@@ -27,7 +27,7 @@
 WIDE = 384
 SEL = ROWS_P + COLS_P
 XY_ORDER = [(dx, dy) for dx in (0, 1, 3, 2) for dy in (0, 1, 3, 2) if dx or dy]
-XY_TARGETS = sorted(((x, y) for x in range(NX) for y in range(NY)), key=lambda p: (2 * p[0] + 3 * p[1], p))
+XY_TARGETS = sorted(((x, y) for x in range(NX) for y in range(NY)), key=lambda p: (p[1] + (p[0] > 0), p))
 Z_ORDER = (0, 1, 2, 3, 7, 4, 6, 5)
 OWNERS = 2
 STRIDE = 3
@@ -243,7 +243,7 @@
     inside = (wide_lane != 0) & (wide_lane != HALF - 1)
 
     def products(k, carry):
-        xx = k
+        xx = k + over(k, 2) - 2 * over(k, 3)
         for yy in range(NY):
             source = 4 * xx + yy
             arrived = pltpu.make_async_remote_copy(

time: 30.9 us -> 30.8 us (level); the launches traced: 30.4 us -> 30.7 us
    pallas_call x1, Pallas kernels: 28.9 us -> 29.2 us  [local(): pl.pallas_call(kernel, out_shape=tuple((f32(*shape) for shape in shapes))...]
where the time goes in v7:
time: 30.8 us; the launch traced here: 30.7 us
  Pallas kernels  30 us (97%)
  between operations  0.64 us (2%)
    pallas_call x1, Pallas kernels, local(): pl.pallas_call(kernel, out_shape=tuple((f32(*shape) for shape in shapes))...  29.2 us
    pallas_call x1, Pallas kernels, local(): pl.pallas_call(write, out_shape=tuple((jax.ShapeDtypeStruct(shape, F32) f...  0.8 us

profile of v7, /device:TPU:1, one launch (start us, length us, event | category | flops | bytes accessed | tf_op | source)
XLA Modules:
  0.0 30.7 jit_solution(1834361313283535793)
XLA Ops:
  0.6 29.2 %shard_map.66 = (f32[64,512]{1,0:T(8,128)S(1)}, f32[64,512]{1,0:T(8,128)S(1)}, f32[67,268]{1,0:T(8,128)S(1)}, f32[64,268]{1,0:T(8,128)S(1)}) custom-call(bf16[512,2048]{1,0:T(8,128)(2,1)} %snap_hbm.1, bf16[64,2048]{1,0:T(8,128)(2,1)} %bitcast.5, f32[2144]{0:T(1024)} %reg_hbm.1), custom_call_target="tpu_custom_call" | custom-call | flops 1073741824 | bytes 3145728 | tf_op jit(solution)/shard_map/pallas_call | solution.py:346
  29.9 0.8 %shard_map.67 = (f32[64,512]{1,0:T(8,128)}, f32[64,512]{1,0:T(8,128)}, f32[67,268]{1,0:T(8,128)}, f32[64,268]{1,0:T(8,128)}) custom-call(f32[64,512]{1,0:T(8,128)S(1)} %get-tuple-element.12.red, f32[64,512]{1,0:T(8,128)S(1)} %get-tuple-element.13.rate, f32[67,268]{1,0:T(8,128)S(1)} %get-tuple-element.14.norm, f32[64,268]{1,0:T(8,128)S(1)} %get-tuple-element.15.rhs), custom_call_target="tpu_custom_call" | custom-call | tf_op jit(solution)/shard_map/pallas_call | solution.py:377
